TPU v7x, 128 devices: a whole 4x4x4 slice. The times are simulated.
128 devices in a mesh: rep: 64 (over z_lo, y, x, core), grp: 2 (over z_hi).
Axes of the slice: x: 4, y: 4, z: 4 (z_hi: 2, z_lo: 2; z = z_hi * 2 + z_lo), core: 2. Of those that a mesh axis runs over, the one named last changes fastest.
Arguments:
- tokens: bfloat16 [32768, 1024], P(('rep', 'grp')), may hold values from -6 to 6
- segments: int32 [32768], P(('rep', 'grp')), may hold values from 1 to 10, as said below
- in_gain: bfloat16 [1024], P('grp'), may hold values from 0.5 to 1.5
- w_in: bfloat16 [1024, 4384], P('grp'), may hold values from -0.1875 to 0.1875
- conv_w: bfloat16 [4, 2304], P(None, 'grp'), may hold values from -3 to 3
- conv_b: bfloat16 [2304], P('grp'), may hold values from -1.5 to 1.5
- dt_bias: bfloat16 [32], P('grp'), may hold values from -6 to -1
- a_log: bfloat16 [32], P('grp'), may hold values from 0 to 2.765625
- d_skip: bfloat16 [32], P('grp'), may hold values from 0.5 to 1.5
- gate_gain: bfloat16 [2048], P('grp'), may hold values from 0.5 to 1.5
- w_out: bfloat16 [2048, 1024], P('grp'), may hold values from -0.125 to 0.125
- cotangent: bfloat16 [32768, 1024], P(('rep', 'grp')), may hold values from -6 to 6
Outputs:
- mixed: bfloat16 [32768, 1024], P(('rep', 'grp'))
- input_grad: float32 [32768, 1024], P(('rep', 'grp'))
- in_gain_grad: float32 [1024], P('grp')
- w_in_grad: float32 [1024, 4384], P('grp')
- conv_w_grad: float32 [4, 2304], P(None, 'grp')
- conv_b_grad: float32 [2304], P('grp')
- dt_bias_grad: float32 [32], P('grp')
- a_log_grad: float32 [32], P('grp')
- d_skip_grad: float32 [32], P('grp')
- gate_gain_grad: float32 [2048], P('grp')
- w_out_grad: float32 [2048, 1024], P('grp')
Inputs may be any that keep to these rules, and one draw needn't show every extreme that they name: `segments`: within each sequence of 512 tokens the numbers start at 1, never fall and rise by one at each new document; documents hold 60 to 800 tokens except where a sequence's start or end cuts them; one document of each sequence holds both tokens 256 - 1 and 256 of it, and in the first sequence that document holds exactly min(800, 512) tokens.
All inputs are finite; a program needn't handle non-finite values.
Results may differ from a plain program's by a relative error of at most 0.0069.
Values may be sent and summed in bfloat16 or wider, within the bound.
A program may use at most 192 MiB of HBM per device.

v0:
```python
import jax
import jax.numpy as jnp
from jax import lax
from jax.sharding import PartitionSpec as P

HEADS = 32
HEAD_DIM = 64
STATE = 128
CONV = 4
STRETCH = 256
INNER = 2048


EPS = 1e-05
HIGHEST = lax.Precision.HIGHEST


def from_behind(block, axis, distance):
    devices = range(lax.axis_size(axis))
    route = [(i - distance, i) for i in devices if i - distance in devices]
    return lax.ppermute(block, axis, route)


def entering(shard, axis, combine, identity):
    length, here = (lax.axis_size(axis), lax.axis_index(axis))
    everything = jax.tree.map(lambda part: lax.all_gather(part, axis), shard)
    start = jax.tree.map(
        lambda part, zero: jnp.broadcast_to(jnp.asarray(zero, part.dtype), part.shape),
        shard,
        identity,
    )

    def entering_step(k, before):
        reached = k < here
        new = combine(before, jax.tree.map(lambda part: part[k], everything))
        return jax.tree.map(lambda a, b: jnp.where(reached, a, b), new, before)

    return lax.fori_loop(0, length, entering_step, start)


def prefix(shard, axis, combine, identity):
    length, here = (lax.axis_size(axis), lax.axis_index(axis))
    everything = jax.tree.map(
        lambda part, kind: lax.all_gather(part.astype(kind), axis),
        shard,
        jax.tree.map(lambda a: jnp.bfloat16 if a.dtype == jnp.float32 else a.dtype, shard),
    )
    start = jax.tree.map(
        lambda part, zero: jnp.broadcast_to(jnp.asarray(zero, part.dtype), part.shape),
        shard,
        identity,
    )

    def prefix_step(k, before):
        at = length - 1 - k
        reached = at > here
        new = combine(
            before, jax.tree.map(lambda part, own: part[at].astype(own.dtype), everything, shard)
        )
        return jax.tree.map(lambda a, b: jnp.where(reached, a, b), new, before)

    return lax.fori_loop(0, length, prefix_step, start)


def prenorm(inputs, gain):
    square = jnp.mean(inputs * inputs, axis=1, keepdims=True)
    return inputs * lax.rsqrt(square + EPS) * gain[None, :]


def mix_inputs(extended, ext_seg, seg_ids, dt_raw, conv_weight, conv_bias, dt_bias, a_log):
    count = seg_ids.shape[0]
    total = jnp.zeros((count, extended.shape[1]), jnp.float32) + conv_bias[None, :]
    for offset in range(CONV):
        rows = extended[offset : offset + count]
        same = (ext_seg[offset : offset + count] == seg_ids).astype(jnp.float32)
        total = total + conv_weight[offset][None, :] * rows * same[:, None]
    active = jax.nn.silu(total)
    head_in = active[:, :INNER].reshape(count, HEADS, HEAD_DIM)
    b_mat = active[:, INNER : INNER + STATE]
    c_mat = active[:, INNER + STATE :]
    step_size = jax.nn.softplus(dt_raw + dt_bias[None, :])
    decay_rate = -jnp.exp(a_log)
    return (head_in, b_mat, c_mat, step_size, decay_rate)


def ssd_block(head_in, b_mat, c_mat, step_size, decay_rate, state, seg_ids, prev_seg):
    log_decay = step_size * decay_rate[None, :]
    running = jnp.cumsum(log_decay, axis=0)
    length = seg_ids.shape[0]
    places = jnp.arange(length)
    allowed = (places[:, None] >= places[None, :]) & (seg_ids[:, None] == seg_ids[None, :])
    spread = running[:, None, :] - running[None, :, :]
    kernel = jnp.where(
        allowed[:, :, None], jnp.exp(jnp.where(allowed[:, :, None], spread, 0.0)), 0.0
    )
    scores = jnp.dot(c_mat, b_mat.T, precision=HIGHEST)
    weights = kernel * scores[:, :, None] * step_size[None, :, :]
    output = jnp.einsum("tsh,shd->thd", weights, head_in, precision=HIGHEST)
    carried = (seg_ids == prev_seg).astype(jnp.float32)
    enter = jnp.exp(running) * carried[:, None]
    output = output + jnp.einsum("tn,hdn->thd", c_mat, state, precision=HIGHEST) * enter[:, :, None]
    tail = (
        jnp.exp(running[-1][None, :] - running)
        * (seg_ids == seg_ids[-1]).astype(jnp.float32)[:, None]
    )
    new_state = jnp.einsum(
        "shd,sn->hdn", head_in * (step_size * tail)[:, :, None], b_mat, precision=HIGHEST
    )
    new_state = new_state + enter[-1][:, None, None] * state
    return (output, new_state, enter)


def gated(ssd_out, head_in, gate_in, skip_weight, norm_gain):
    count = ssd_out.shape[0]
    full = (ssd_out + skip_weight[None, :, None] * head_in).reshape(count, INNER)
    gated_val = full * jax.nn.silu(gate_in)
    square = jnp.mean(gated_val * gated_val, axis=1, keepdims=True)
    return gated_val * lax.rsqrt(square + EPS) * norm_gain[None, :]


def chain(earlier, later):
    return (earlier[0] * later[0], later[1] + later[0][:, None, None] * earlier[1])


def on_device(
    tokens,
    segments,
    in_gain,
    w_in,
    conv_w,
    conv_b,
    dt_bias,
    a_log,
    d_skip,
    gate_gain,
    w_out,
    cotangent,
):
    gathered = (
        lax.all_gather(w_in, "grp", axis=0, tiled=True),
        lax.all_gather(conv_w, "grp", axis=1, tiled=True),
        lax.all_gather(conv_b, "grp", axis=0, tiled=True),
        lax.all_gather(dt_bias, "grp", axis=0, tiled=True),
        lax.all_gather(a_log, "grp", axis=0, tiled=True),
        lax.all_gather(d_skip, "grp", axis=0, tiled=True),
        lax.all_gather(gate_gain, "grp", axis=0, tiled=True),
        lax.all_gather(in_gain, "grp", axis=0, tiled=True),
        lax.all_gather(w_out, "grp", axis=0, tiled=True),
    )
    full_in = gathered[0]
    full_out = gathered[8]
    conv_weight = gathered[1].astype(jnp.float32)
    conv_bias = gathered[2].astype(jnp.float32)
    bias_full = gathered[3].astype(jnp.float32)
    alog_full = gathered[4].astype(jnp.float32)
    skip_full = gathered[5].astype(jnp.float32)
    ggain_full = gathered[6].astype(jnp.float32)
    igain_full = gathered[7].astype(jnp.float32)
    inputs = tokens.astype(jnp.float32)
    count = inputs.shape[0]
    normed, pre_pull = jax.vjp(prenorm, inputs, igain_full)
    normed_low = normed.astype(jnp.bfloat16)
    proj = jnp.dot(normed_low, full_in, preferred_element_type=jnp.float32)
    gate_in = proj[:, :INNER]
    conv_in = proj[:, INNER : INNER + INNER + 2 * STATE]
    dt_raw = proj[:, INNER + INNER + 2 * STATE :]
    rim = CONV - 1
    edge_rows, edge_seg = from_behind(
        (conv_in[count - rim :], segments[count - rim :].astype(jnp.float32)), "grp", 1
    )
    prev_seg = edge_seg.astype(jnp.int32)
    extended = jnp.concatenate([edge_rows, conv_in], axis=0)
    ext_seg = jnp.concatenate([prev_seg, segments])

    def mixing(ext_rows, raw_steps, weight_taps, bias_taps, bias_steps, log_rates):
        return mix_inputs(
            ext_rows, ext_seg, segments, raw_steps, weight_taps, bias_taps, bias_steps, log_rates
        )

    mixed_out, mix_pull = jax.vjp(
        mixing, extended, dt_raw, conv_weight, conv_bias, bias_full, alog_full
    )
    head_in, b_mat, c_mat, step_size, decay_rate = mixed_out
    width = min(STRETCH, count)
    blocks = count // width
    head_blocks = head_in.reshape(blocks, width, HEADS, HEAD_DIM)
    b_blocks = b_mat.reshape(blocks, width, STATE)
    c_blocks = c_mat.reshape(blocks, width, STATE)
    step_blocks = step_size.reshape(blocks, width, HEADS)
    seg_blocks = segments.reshape(blocks, width)
    prev_blocks = jnp.concatenate([prev_seg[rim - 1 :], seg_blocks[:-1, -1]])

    def advance(carry, pieces):
        state, factor = carry
        head_part, b_part, c_part, step_part, seg_part, prev_part = pieces
        output, new_state, enter = ssd_block(
            head_part, b_part, c_part, step_part, decay_rate, state, seg_part, prev_part
        )
        return ((new_state, factor * enter[-1]), (output, state, factor, enter))

    zero_state = jnp.zeros((HEADS, HEAD_DIM, STATE), jnp.float32)
    unit_factor = jnp.ones((HEADS,), jnp.float32)
    (local_state, piece_factor), (partial_value, starts_zero, factors, enters) = lax.scan(
        advance,
        (zero_state, unit_factor),
        (head_blocks, b_blocks, c_blocks, step_blocks, seg_blocks, prev_blocks),
    )
    incoming = entering((piece_factor, local_state), "grp", chain, (unit_factor, zero_state))[1]
    starts = starts_zero + factors[:, :, None, None] * incoming[None]
    weight_in = enters * factors[:, None, :]
    ssd_out = (
        partial_value
        + jnp.einsum("btn,hdn->bthd", c_blocks, incoming, precision=HIGHEST) * weight_in[..., None]
    )
    ssd_out = ssd_out.reshape(count, HEADS, HEAD_DIM)
    branch, gate_pull = jax.vjp(gated, ssd_out, head_in, gate_in, skip_full, ggain_full)
    branch_low = branch.astype(jnp.bfloat16)
    mixed = (inputs + jnp.dot(branch_low, full_out, preferred_element_type=jnp.float32)).astype(
        jnp.bfloat16
    )
    again = (
        lax.all_gather(w_in, "grp", axis=0, tiled=True),
        lax.all_gather(w_out, "grp", axis=0, tiled=True),
    )
    back_in = again[0]
    back_out = again[1]
    out_grad = jnp.dot(branch_low.T, cotangent, preferred_element_type=jnp.float32)
    branch_grad = jnp.dot(cotangent, back_out.T, preferred_element_type=jnp.float32)
    ssd_grad, head_gate_grad, gate_in_grad, skip_grad, ggain_grad = gate_pull(branch_grad)
    ssd_grad_blocks = ssd_grad.reshape(blocks, width, HEADS, HEAD_DIM)
    local_grad = jnp.einsum(
        "bth,bthd,btn->hdn", weight_in, ssd_grad_blocks, c_blocks, precision=HIGHEST
    )
    end_grad = prefix((piece_factor, local_grad), "grp", chain, (unit_factor, zero_state))[1]

    def retreat(carry, pieces):
        head_part, b_part, c_part, step_part, seg_part, prev_part, start_part, grad_part = pieces

        def local_block(head_val, b_val, c_val, step_val, rate_val, state_val):
            result = ssd_block(
                head_val, b_val, c_val, step_val, rate_val, state_val, seg_part, prev_part
            )
            return (result[0], result[1])

        _, block_pull = jax.vjp(
            local_block, head_part, b_part, c_part, step_part, decay_rate, start_part
        )
        grads = block_pull((grad_part, carry))
        return (grads[5], grads[:5])

    _, block_grads = lax.scan(
        retreat,
        end_grad,
        (
            head_blocks,
            b_blocks,
            c_blocks,
            step_blocks,
            seg_blocks,
            prev_blocks,
            starts,
            ssd_grad_blocks,
        ),
        reverse=True,
    )
    head_grad = block_grads[0].reshape(count, HEADS, HEAD_DIM) + head_gate_grad
    b_grad = block_grads[1].reshape(count, STATE)
    c_grad = block_grads[2].reshape(count, STATE)
    step_grad = block_grads[3].reshape(count, HEADS)
    rate_grad = jnp.sum(block_grads[4], axis=0)
    ext_grad, raw_grad, conv_w_grad, conv_b_grad, bias_grad, alog_grad = mix_pull(
        (head_grad, b_grad, c_grad, step_grad, rate_grad)
    )
    returned = from_behind(ext_grad[:rim], "grp", -1)
    conv_in_grad = ext_grad[rim:] + jnp.pad(returned, ((count - rim, 0), (0, 0)))
    proj_grad = jnp.concatenate([gate_in_grad, conv_in_grad, raw_grad], axis=1).astype(jnp.bfloat16)
    in_grad = jnp.dot(normed_low.T, proj_grad, preferred_element_type=jnp.float32)
    normed_grad = jnp.dot(proj_grad, back_in.T, preferred_element_type=jnp.float32)
    branch_inputs, igain_grad = pre_pull(normed_grad)
    input_grad = cotangent.astype(jnp.float32) + branch_inputs
    summed = (
        lax.psum_scatter(igain_grad, "grp", scatter_dimension=0, tiled=True),
        lax.psum_scatter(in_grad, "grp", scatter_dimension=0, tiled=True),
        lax.psum_scatter(conv_w_grad, "grp", scatter_dimension=1, tiled=True),
        lax.psum_scatter(conv_b_grad, "grp", scatter_dimension=0, tiled=True),
        lax.psum_scatter(bias_grad, "grp", scatter_dimension=0, tiled=True),
        lax.psum_scatter(alog_grad, "grp", scatter_dimension=0, tiled=True),
        lax.psum_scatter(skip_grad, "grp", scatter_dimension=0, tiled=True),
        lax.psum_scatter(ggain_grad, "grp", scatter_dimension=0, tiled=True),
        lax.psum_scatter(out_grad, "grp", scatter_dimension=0, tiled=True),
    )
    summed = lax.psum(
        (
            summed[0],
            summed[1],
            summed[2],
            summed[3],
            summed[4],
            summed[5],
            summed[6],
            summed[7],
            summed[8],
        ),
        "rep",
    )
    return (
        mixed,
        input_grad,
        summed[0],
        summed[1],
        summed[2],
        summed[3],
        summed[4],
        summed[5],
        summed[6],
        summed[7],
        summed[8],
    )


def solution(mesh):
    placed = (
        P(("rep", "grp"), None),
        P(("rep", "grp")),
        P("grp"),
        P("grp", None),
        P(None, "grp"),
        P("grp"),
        P("grp"),
        P("grp"),
        P("grp"),
        P("grp"),
        P("grp", None),
        P(("rep", "grp"), None),
    )
    return jax.shard_map(
        on_device,
        mesh=mesh,
        in_specs=placed,
        out_specs=(
            P(("rep", "grp"), None),
            P(("rep", "grp"), None),
            P("grp"),
            P("grp", None),
            P(None, "grp"),
            P("grp"),
            P("grp"),
            P("grp"),
            P("grp"),
            P("grp"),
            P("grp", None),
        ),
        check_vma=False,
    )
```

profile of v0, /device:TPU:1, one launch (start us, length us, event | category | flops | bytes accessed | tf_op | source)
XLA Modules:
  0.0 1248.5 jit_solution(5597889587213674168)
XLA Ops:
  8.1 6.3 collective-permute-start.1
  15.1 4.7 all-gather.3
  19.8 4.7 all_gather.50
  24.5 4.7 all-gather.2
  31.9 6.2 all-reduce.26
  40.2 1.9 compare_convert_fusion.4
  42.2 88.1 %all-gather.11.cloned.1.call-done = bf16[1024,4384]{0,1:T(8,128)(2,1)} async-done(((bf16[512,4384]{0,1:T(8,128)(2,1)}), bf16[1024,4384]{0,1:T(8,128)(2,1)}) %all-gather.11.cloned.1.call-update) | async-done | bytes 8978448 | tf_op jit(solution)/shard_map/all_gather | solution.py:140
  130.3 6.4 fusion.73
  136.7 2.0 copy-done.6
  144.3 3.3 slice.127
  149.1 10.5 fusion.29
  159.7 1.9 copy-done.11
  161.6 2.8 fusion.45
  166.7 4.7 all_gather.59
  172.9 5.0 all-gather.4
  179.0 3.1 fusion.68
  182.2 20.1 %all-gather.15.cloned.1.call-done = f32[64,64,128]{2,1,0:T(8,128)} async-done(((f32[32,64,128]{2,1,0:T(8,128)}), f32[64,64,128]{2,1,0:T(8,128)}) %all-gather.15.cloned.1.call-update) | async-done | bytes 2097168 | tf_op jit(solution)/shard_map/all_gather | solution.py:26
  202.3 5.2 while.20
  209.3 11.7 fusion.33
  221.1 3.8 multiply_reduce_fusion.10
  226.0 38.1 %all-gather.13.cloned.1.call-done = bf16[2048,1024]{1,0:T(8,128)(2,1)} async-done(((bf16[1024,1024]{1,0:T(8,128)(2,1)}), bf16[2048,1024]{1,0:T(8,128)(2,1)}) %all-gather.13.cloned.1.call-update) | async-done | bytes 4194320 | tf_op jit(solution)/shard_map/all_gather | solution.py:148
  264.1 5.4 multiply_reduce_fusion.5
  269.5 4.5 multiply_reduce_fusion.6
  275.4 2.6 fusion.49
  278.2 6.4 fusion.109
  284.9 4.7 all-gather.5
  289.6 2.7 multiply_reduce_fusion.7
  292.3 14.0 %fusion.11 = (f32[256,32]{0,1:T(8,128)S(1)}, f32[256,32]{0,1:T(8,128)S(1)}, f32[256,32]{0,1:T(8,128)}, f32[256,256]{1,0:T(8,128)S(1)}) fusion(f32[256,32]{0,1:T(8,128)S(1)} %get-tuple-element.430, f32[256,256]{1,0:T(8,128)S(1)} %copy-done.37, f32[256,32]{0,1:T(8,128)S(1)} %copy-done.48, pred[256,256]{1,0:T(8,128)(4,1)S(1)} %copy-done.50, ...), kind=kOutput, calls=%fused_computation.20 | convolution fusion | flops 1641979904 | bytes 4947968 | tf_op jit(solution)/shard_map/while/body/eval_jaxpr/transpose(jvp(tsh,shd->thd))/dot_general | solution.py:98
  306.4 2.7 while.21
  309.5 4.8 multiply_reduce_fusion.8
  314.7 2.5 reduce-window.24
  318.0 9.5 bitcast_add_fusion.2
  327.9 1.9 convolution_bitcast_fusion
  329.9 2.0 fusion.54
  334.5 7.2 multiply_reduce_fusion.3
  349.8 7.9 pad_add_fusion
  359.2 2.9 fusion.28
  362.2 8.8 fusion.66
  373.4 35.8 %reduce-scatter.8.cloned.1.call-done = f32[1024,1024]{1,0:T(8,128)} async-done(((f32[2048,1024]{1,0:T(8,128)}), f32[1024,1024]{1,0:T(8,128)}) %reduce-scatter.8.cloned.1.call-update) | async-done | bytes 4194320 | tf_op jit(solution)/shard_map/reduce_scatter | solution.py:290
  409.1 207.2 %reduce-scatter.6.cloned.1.call-done = f32[512,4384]{0,1:T(8,128)} async-done(((f32[1024,4384]{0,1:T(8,128)}), f32[512,4384]{0,1:T(8,128)}) %reduce-scatter.6.cloned.1.call-update) | async-done | bytes 8978448 | tf_op jit(solution)/shard_map/reduce_scatter | solution.py:283
  619.4 4.6 fusion.48
  624.0 6.5 fusion.58
  630.5 8.1 all-reduce.25
  640.3 4.9 reduce-scatter.10.cloned.1.call-done
  646.5 273.6 %all-reduce.23 = (f32[512]{0:T(512)}, f32[4,1152]{1,0:T(4,128)}, f32[1152]{0:T(1024)}, f32[16]{0:T(128)}, f32[16]{0:T(128)}, /*index=5*/f32[16]{0:T(128)}, f32[1024]{0:T(1024)}) all-reduce(f32[512]{0:T(512)S(1)} %dynamic-slice.12, f32[4,1152]{1,0:T(4,128)S(1)} %copy.117, ...), channel_id=1, replica_groups=mesh['rep'=64,'grp'=2] {'rep'}, use_global_device_ids=true, to_apply=%region_22.23 | all-reduce | flops 7344 | bytes 58752 | tf_op jit(solution)/shard_map/psum | solution.py:292
  920.2 310.7 %all-reduce.29.cloned.1.call-done = (f32[512,4384]{0,1:T(8,128)}, f32[1024,1024]{1,0:T(8,128)}) async-done(((f32[512,4384]{0,1:T(8,128)}, f32[1024,1024]{1,0:T(8,128)}), (f32[512,4384]{0,1:T(8,128)}, f32[1024,1024]{1,0:T(8,128)})) %all-reduce.29.cloned.1.call-update) | async-done | bytes 13172752 | tf_op jit(solution)/shard_map/psum | solution.py:292
  1230.8 8.4 copy.161
  1239.2 2.0 copy.162
  (319 shorter events, 49.4 us)
Async XLA Ops:
  7.2 22.7 %copy-start.96 = (u32[128]{0:T(128)S(1)}, u32[128]{0:T(128)}, u32[]{:S(2)}) copy-start(u32[128]{0:T(128)} %constant.178) | copy-start | bytes 1540
  7.2 12.5 %copy-start.87 = (bf16[4,1152]{1,0:T(4,128)(2,1)S(1)}, bf16[4,1152]{1,0:T(4,128)(2,1)}, u32[]{:S(2)}) copy-start(bf16[4,1152]{1,0:T(4,128)(2,1)} %param.20) | copy-start | bytes 27652
  7.2 17.3 %copy-start.90 = (bf16[1152]{0:T(1024)(128)(2,1)S(1)}, bf16[1152]{0:T(1024)(128)(2,1)}, u32[]{:S(2)}) copy-start(bf16[1152]{0:T(1024)(128)(2,1)} %param.21) | copy-start | bytes 6916
  7.2 23.9 %copy-start.99 = (bf16[16]{0:T(256)(128)(2,1)S(1)}, bf16[16]{0:T(256)(128)(2,1)}, u32[]{:S(2)}) copy-start(bf16[16]{0:T(256)(128)(2,1)} %param.24) | copy-start | bytes 100
  7.2 24.1 %copy-start.100 = (bf16[16]{0:T(256)(128)(2,1)S(1)}, bf16[16]{0:T(256)(128)(2,1)}, u32[]{:S(2)}) copy-start(bf16[16]{0:T(256)(128)(2,1)} %param.22) | copy-start | bytes 100
  7.3 24.4 %copy-start.101 = (bf16[16]{0:T(256)(128)(2,1)S(1)}, bf16[16]{0:T(256)(128)(2,1)}, u32[]{:S(2)}) copy-start(bf16[16]{0:T(256)(128)(2,1)} %param.23) | copy-start | bytes 100
  7.3 31.5 %copy-start.20 = (bf16[256,1024]{1,0:T(8,128)(2,1)S(1)}, bf16[256,1024]{1,0:T(8,128)(2,1)}, u32[]{:S(2)}) copy-start(bf16[256,1024]{1,0:T(8,128)(2,1)} %param.16) | copy-start | bytes 1572868
  7.3 123.0 %all-gather.11.cloned.1.call-start = ((), (), s32[]{:S(2)}) async-start(), calls=%async_computation.3 | async-start | bytes 13467648 | tf_op jit(solution)/shard_map/all_gather | solution.py:140
  8.0 194.2 %all-gather.15.cloned.1.call-start = ((), (), s32[]{:S(2)}) async-start(), calls=%async_computation.7 | async-start | bytes 3145728 | tf_op jit(solution)/shard_map/all_gather | solution.py:26
  8.1 30.9 %collective-permute-start.1 = (f32[3]{0:T(128)S(1)}, f32[3]{0:T(128)S(1)}, u32[]{:S(2)}, u32[]{:S(2)}) collective-permute-start(f32[3]{0:T(128)S(1)} %slice_convert_fusion.1), channel_id=1, source_target_pairs={{0,1},{2,3},{4,5},{6,7},{8,9},{10,11},{12,13},{14,15},{16,17},{18,... | collective-permute-start | bytes 44 | tf_op jit(solution)/shard_map/ppermute | solution.py:21
  19.7 110.5 %copy-start.60 = (f32[2,1,512]{2,1,0:T(1,128)}, f32[2,1,512]{2,1,0:T(1,128)S(1)}, u32[]{:S(2)}) copy-start(f32[2,1,512]{2,1,0:T(1,128)S(1)} %convert_element_type.127) | copy-start | bytes 12292
  38.1 103.0 %copy-start.91 = (f32[32]{0:T(128)}, f32[32]{0:T(128)S(1)}, u32[]{:S(2)}) copy-start(f32[32]{0:T(128)S(1)} %convert_element_type.113) | copy-start | bytes 388
  38.8 110.2 %copy-start.38 = (f32[2304]{0:T(1024)}, f32[2304]{0:T(1024)S(1)}, u32[]{:S(2)}) copy-start(f32[2304]{0:T(1024)S(1)} %get-tuple-element.378) | copy-start | bytes 27652
  39.0 102.1 %copy-start.93 = (f32[32]{0:T(128)}, f32[32]{0:T(128)S(1)}, u32[]{:S(2)}) copy-start(f32[32]{0:T(128)S(1)} %fusion.102) | copy-start | bytes 388
  39.0 91.2 %copy-start.81 = (f32[256]{0:T(256)}, f32[256]{0:T(256)S(1)}, u32[]{:S(2)}) copy-start(f32[256]{0:T(256)S(1)} %fusion.100) | copy-start | bytes 3076
  42.2 101.3 %copy-start.64 = (f32[256]{0:T(256)}, f32[256]{0:T(256)S(1)}, u32[]{:S(2)}) copy-start(f32[256]{0:T(256)S(1)} %get-tuple-element.447) | copy-start | bytes 3076
  42.2 101.3 %copy-start.79 = (f32[256]{0:T(256)}, f32[256]{0:T(256)S(1)}, u32[]{:S(2)}) copy-start(f32[256]{0:T(256)S(1)} %get-tuple-element.446) | copy-start | bytes 3076
  42.2 106.9 %copy-start.70 = (f32[256]{0:T(256)}, f32[256]{0:T(256)S(1)}, u32[]{:S(2)}) copy-start(f32[256]{0:T(256)S(1)} %get-tuple-element.443) | copy-start | bytes 3076
  139.4 8.1 collective-permute-start
  141.9 176.0 %copy-start.30 = (f32[256,32]{0,1:T(8,128)}, f32[256,32]{0,1:T(8,128)S(1)}, u32[]{:S(2)}) copy-start(f32[256,32]{0,1:T(8,128)S(1)} %get-tuple-element.430) | copy-start | bytes 98308
  142.6 172.1 %copy-start.28 = (f32[32,2,128]{2,0,1:T(8,128)}, f32[32,2,128]{2,0,1:T(8,128)S(1)}, u32[]{:S(2)}) copy-start(f32[32,2,128]{2,0,1:T(8,128)S(1)} %reduce-window.16) | copy-start | bytes 98308
  159.6 114.5 %copy-start = (f32[256,2304]{0,1:T(8,128)}, f32[256,2304]{0,1:T(8,128)S(1)}, u32[]{:S(2)}) copy-start(f32[256,2304]{0,1:T(8,128)S(1)} %get-tuple-element.431) | copy-start | bytes 7077892
  164.4 99.7 %all-gather.13.cloned.1.call-start = ((), (), s32[]{:S(2)}) async-start(), calls=%async_computation.4 | async-start | bytes 6291456 | tf_op jit(solution)/shard_map/all_gather | solution.py:148
  165.1 141.2 %all-gather.17.cloned.1.call-start = ((), (), s32[]{:S(2)}) async-start(), calls=%async_computation.8 | async-start | bytes 1572864 | tf_op jit(solution)/shard_map/all_gather | solution.py:44
  209.3 11.7 copy-start.19
  278.0 131.1 %reduce-scatter.8.cloned.1.call-start = ((), (), s32[]{:S(2)}) async-start(), calls=%async_computation.6 | async-start | bytes 12582912 | tf_op jit(solution)/shard_map/reduce_scatter | solution.py:290
  284.6 331.7 %reduce-scatter.6.cloned.1.call-start = ((), (), s32[]{:S(2)}) async-start(), calls=%async_computation.5 | async-start | bytes 26935296 | tf_op jit(solution)/shard_map/reduce_scatter | solution.py:283
  314.3 13.1 %copy-start.32 = (f32[256,32]{0,1:T(8,128)}, f32[256,32]{0,1:T(8,128)S(1)}, u32[]{:S(2)}) copy-start(f32[256,32]{0,1:T(8,128)S(1)} %get-tuple-element.451) | copy-start | bytes 98308
  317.3 10.2 copy-start.34
  318.0 9.5 copy-start.3
  348.0 9.7 copy-start.29
  348.0 9.7 copy-start.31
  348.0 9.7 copy-start.33
  348.0 9.7 copy-start.35
  348.0 9.7 copy-start.59
  348.1 9.7 copy-start.63
  348.1 9.7 copy-start.66
  348.1 9.7 copy-start.78
  348.1 9.7 copy-start.89
  348.1 9.7 copy-start.92
  348.1 9.7 copy-start.94
  348.1 10.7 collective-permute-start.2
  371.1 274.2 %reduce-scatter.10.cloned.1.call-start = ((), (), s32[]{:S(2)}) async-start(), calls=%async_computation.9 | async-start | bytes 1769472
  373.3 857.5 %all-reduce.29.cloned.1.call-start = ((), (), s32[]{:S(2)}) async-start(), calls=%async_computation.10 | async-start | bytes 26345472 | tf_op jit(solution)/shard_map/psum | solution.py:292
  624.0 15.0 %copy-start.84 = (f32[256]{0:T(256)S(1)}, f32[256]{0:T(256)}, u32[]{:S(2)}) copy-start(f32[256]{0:T(256)} %copy-done.83) | copy-start | bytes 3076
  624.0 15.0 %copy-start.23 = (bf16[256,1024]{1,0:T(8,128)(2,1)S(1)}, bf16[256,1024]{1,0:T(8,128)(2,1)}, u32[]{:S(2)}) copy-start(bf16[256,1024]{1,0:T(8,128)(2,1)} %param.16) | copy-start | bytes 1572868
  624.0 15.0 %copy-start.27 = (bf16[256,1024]{1,0:T(8,128)(2,1)S(1)}, bf16[256,1024]{1,0:T(8,128)(2,1)}, u32[]{:S(2)}) copy-start(bf16[256,1024]{1,0:T(8,128)(2,1)} %param.27) | copy-start | bytes 1572868
  1230.8 8.4 copy-start.26
  (67 other events, 259.7 us)
Sparse Core Ops, SparseCore 0:
  9.8 120.4 all-gather.10
  164.5 37.6 all-gather.14
  203.9 60.1 all-gather.12
  278.1 24.6 all-gather.16
  305.7 103.4 reduce-scatter.7
  411.5 204.7 reduce-scatter.5
  619.4 25.8 reduce-scatter.9
  647.9 582.9 all-reduce.28
where the time goes:
time: 1260 us; the launch traced here: 1250 us
  waiting for transfers between devices  706 us (56%)
  blocking collectives  316 us (25%)
  matrix products  96 us (8%)
  other arithmetic  60.1 us (5%)
  local copies, waits for them, and re-layouts  40 us (3%)
  between operations  19.3 us (2%)
    psum x1, waiting for transfers between devices, on_device(): lax.psum((summed[0], summed[1], summed[2], summed[3], summed[4], summed[5...  311 us
    psum x1, blocking collectives, on_device(): lax.psum((summed[0], summed[1], summed[2], summed[3], summed[4], summed[5...  274 us
    reduce_scatter x1, waiting for transfers between devices, on_device(): lax.psum_scatter(in_grad, 'grp', scatter_dimension=0, tiled=True)  207 us
    all_gather x1, waiting for transfers between devices, on_device(): lax.all_gather(w_in, 'grp', axis=0, tiled=True)  88.1 us
    all_gather x1, waiting for transfers between devices, on_device(): lax.all_gather(w_out, 'grp', axis=0, tiled=True)  38.1 us
    reduce_scatter x1, waiting for transfers between devices, on_device(): lax.psum_scatter(out_grad, 'grp', scatter_dimension=0, tiled=True)  35.8 us
    dot_general x3, matrix products, ssd_block(): output = jnp.einsum('tsh,shd->thd', weights, head_in, precision=HIGHEST)  35.2 us
    unnamed x228, local copies, waits for them, and re-layouts  25.4 us
  transfers between devices with their start and end apart: 11, of which 7 were waited for; matrix products, arithmetic and copies ran while one was open for 11% of the time, Pallas kernels for 0%

commit v1 on v0

--- a/solution.py
+++ b/solution.py
@@ -1,6 +1,8 @@
 import jax
 import jax.numpy as jnp
 from jax import lax
+from jax.experimental import pallas as pl
+from jax.experimental.pallas import tpu as pltpu
 from jax.sharding import PartitionSpec as P
 
 HEADS = 32
@@ -120,6 +122,413 @@
 
 def chain(earlier, later):
     return (earlier[0] * later[0], later[1] + later[0][:, None, None] * earlier[1])
+
+
+MESH = pl.DeviceIdType.MESH
+RIM = 4
+LANES = 128
+W_IN_COLS = 4608
+PARTS = (
+    ("x", "y", "z", 0, 1152),
+    ("y", "z", "x", 1152, 1152),
+    ("z", "x", "y", 2304, 1024),
+)
+OWN_COLS = 3328
+ALL_COLS = 6656
+N_SEMS = 128
+
+
+def place():
+    rep, grp = lax.axis_index("rep"), lax.axis_index("grp")
+    here = {
+        "core": lax.rem(rep, 2),
+        "x": lax.rem(lax.div(rep, 2), 4),
+        "y": lax.rem(lax.div(rep, 8), 4),
+        "z": 2 * grp + lax.div(rep, 32),
+    }
+    return here
+
+
+def device_at(here):
+    low_z = lax.rem(here["z"], 2)
+    rep = ((low_z * 4 + here["y"]) * 4 + here["x"]) * 2 + here["core"]
+    return (rep, lax.div(here["z"], 2))
+
+
+def moved(here, axis, by):
+    there = dict(here)
+    there[axis] = lax.rem(here[axis] + (by % 4), 4)
+    return there
+
+
+def other_core(here):
+    there = dict(here)
+    there["core"] = 1 - here["core"]
+    return there
+
+
+def greet(partners):
+    barrier = pltpu.get_barrier_semaphore()
+    for partner in partners:
+        pl.semaphore_signal(barrier, inc=1, device_id=partner, device_id_type=MESH)
+    pl.semaphore_wait(barrier, len(partners))
+
+
+class Copies:
+    def __init__(self, send_sems, recv_sems):
+        self.send_sems, self.recv_sems = send_sems, recv_sems
+        self.made = []
+
+    def start(self, src, dst, device):
+        at = len(self.made)
+        copy = pltpu.make_async_remote_copy(
+            src_ref=src,
+            dst_ref=dst,
+            send_sem=self.send_sems.at[at],
+            recv_sem=self.recv_sems.at[at],
+            device_id=device,
+            device_id_type=MESH,
+        )
+        copy.start()
+        self.made.append(copy)
+        return copy
+
+    def finish(self):
+        for copy in self.made:
+            copy.wait_send()
+
+
+def view(ref, axes, cols):
+    return ref.at[axes["x"], axes["y"], axes["z"], :, cols]
+
+
+def halves(axes, free, sizes):
+    if not free:
+        return (axes, None)
+    name = free[0]
+    half = sizes[name] // 2
+    return (
+        dict(axes, **{name: slice(0, half)}),
+        dict(axes, **{name: slice(half, 2 * half)}),
+    )
+
+
+def reduce_kernel(
+    normed_ref,
+    pg_ref,
+    branch_ref,
+    cot_ref,
+    strip_ref,
+    out_ref,
+    far_normed,
+    far_pg,
+    far_branch,
+    far_cot,
+    far_strip,
+    buf,
+    half_a,
+    half_b,
+    half_c,
+    whole_a,
+    whole_b,
+    whole_c,
+    half_a1,
+    half_b1,
+    half_c1,
+    whole_a1,
+    whole_b1,
+    whole_c1,
+    last_a,
+    last_b,
+    last_c,
+    send_sems,
+    recv_sems,
+):
+    here = place()
+    core = here["core"]
+    twin = device_at(other_core(here))
+    greet(
+        [twin]
+        + [device_at(moved(here, axis, by)) for axis in ("x", "y", "z") for by in (1, -1)]
+    )
+    copies = Copies(send_sems, recv_sems)
+
+    theirs = 1 - core
+    branch_in = []
+    for half in range(2):
+        cols = pl.ds(pl.multiple_of(1024 * half + 512 * theirs, 512), 512)
+        branch_in.append(
+            copies.start(branch_ref.at[:, cols], far_branch.at[:, pl.ds(512 * half, 512)], twin)
+        )
+    cot_in = copies.start(cot_ref, far_cot, twin)
+    normed_in = copies.start(normed_ref, far_normed, twin)
+    pg_in = []
+    for part in range(2):
+        cols = pl.ds(pl.multiple_of(2304 * part + 1152 * theirs, 128), 1152)
+        pg_in.append(
+            copies.start(pg_ref.at[:, cols], far_pg.at[:, pl.ds(1152 * part, 1152)], twin)
+        )
+    strip_in = copies.start(strip_ref, far_strip, twin)
+
+    half_in = ((half_a, half_b, half_c), (half_a1, half_b1, half_c1))
+    whole_in = ((whole_a, whole_b, whole_c), (whole_a1, whole_b1, whole_c1), (last_a, last_b, last_c))
+    sizes = {"x": 4, "y": 4, "z": 4}
+
+    def product(left, right):
+        return lax.dot_general(
+            left, right, (((0,), (0,)), ((), ())), preferred_element_type=jnp.float32
+        )
+
+    def store(row, half, cols, value):
+        buf[row, :, 2 * half : 2 * half + 2, :, cols] = value.astype(jnp.bfloat16).reshape(
+            4, 2, 16, value.shape[1]
+        )
+
+    def stage_axes(part, stage):
+        order = PARTS[part][:3]
+        axes = {}
+        for done in order[:stage]:
+            axes[done] = here[done]
+        free = [name for name in ("x", "y", "z") if name in order[stage + 1 :]]
+        for name in free:
+            axes[name] = slice(None)
+        return order[stage], axes, free
+
+    live = {}
+
+    def begin(part, stage):
+        axis, axes, free = stage_axes(part, stage)
+        cols = pl.ds(PARTS[part][3], PARTS[part][4])
+        chunk = lambda by: dict(axes, **{axis: lax.rem(here[axis] + (by % 4), 4)})
+        ahead, behind = device_at(moved(here, axis, 1)), device_at(moved(here, axis, -1))
+        whole = whole_in[stage][part]
+        state = {}
+        far_first, far_second = halves(chunk(2), free, sizes)
+        if stage < 2:
+            halved = half_in[stage][part]
+            state["a"] = copies.start(view(buf, far_first, cols), halved.at[0], ahead)
+            state["b"] = copies.start(view(buf, far_second, cols), halved.at[1], behind)
+            low = lambda ref, d: ref.at[d, pl.ds(0, 2)]
+            high = lambda ref, d: ref.at[d, pl.ds(2, 2)]
+            first, second = halves(chunk(1), free, sizes)
+            state["up_free"] = copies.start(view(buf, second, cols), high(whole, 0), ahead)
+            first, second = halves(chunk(-1), free, sizes)
+            state["down_free"] = copies.start(view(buf, first, cols), low(whole, 1), behind)
+        else:
+            state["a"] = copies.start(view(buf, far_first, cols), whole.at[2], ahead)
+            state["down"] = copies.start(view(buf, chunk(-1), cols), whole.at[1], behind)
+        live[part, stage] = state
+
+    def add_into(axes, cols, incoming):
+        at = (axes["x"], axes["y"], axes["z"], slice(None), cols)
+        total = buf[at].astype(jnp.float32)
+        for value in incoming:
+            total = total + value.astype(jnp.float32)
+        buf[at] = total.astype(jnp.bfloat16)
+
+    def relay(part, stage):
+        axis, axes, free = stage_axes(part, stage)
+        cols = pl.ds(PARTS[part][3], PARTS[part][4])
+        chunk = lambda by: dict(axes, **{axis: lax.rem(here[axis] + (by % 4), 4)})
+        ahead, behind = device_at(moved(here, axis, 1)), device_at(moved(here, axis, -1))
+        whole = whole_in[stage][part]
+        state = live[part, stage]
+        state["a"].wait_recv()
+        if stage < 2:
+            halved = half_in[stage][part]
+            first, _ = halves(chunk(1), free, sizes)
+            add_into(first, cols, [halved[0]])
+            state["up"] = copies.start(view(buf, first, cols), whole.at[0, pl.ds(0, 2)], ahead)
+            state["b"].wait_recv()
+            _, second = halves(chunk(-1), free, sizes)
+            add_into(second, cols, [halved[1]])
+            state["down"] = copies.start(view(buf, second, cols), whole.at[1, pl.ds(2, 2)], behind)
+        else:
+            add_into(chunk(1), cols, [whole[2]])
+            state["up"] = copies.start(view(buf, chunk(1), cols), whole.at[0], ahead)
+
+    def settle(part, stage):
+        axis, axes, free = stage_axes(part, stage)
+        cols = pl.ds(PARTS[part][3], PARTS[part][4])
+        whole = whole_in[stage][part]
+        state = live[part, stage]
+        for name in ("up_free", "down_free", "down", "up"):
+            if name in state:
+                state[name].wait_recv()
+        mine = dict(axes, **{axis: here[axis]})
+        if stage < 2:
+            add_into(mine, cols, [whole[0], whole[1]])
+        else:
+            at = (mine["x"], mine["y"], mine["z"], slice(None), cols)
+            total = buf[at].astype(jnp.float32)
+            total = total + whole[0].astype(jnp.float32) + whole[1].astype(jnp.float32)
+            low_z = lax.rem(here["z"], 2)
+            out_ref[here["x"], here["y"], low_z, :, out_cols(part)] = total.astype(jnp.bfloat16)
+
+    def out_cols(part):
+        start, width = PARTS[part][3:]
+        return pl.ds(pl.multiple_of(2 * start + width * core, LANES), width)
+
+    mine = core
+
+    for copy in branch_in:
+        copy.wait_recv()
+    cot_in.wait_recv()
+    for half in range(2):
+
+        @pl.loop(0, 4)
+        def _(row):
+            near = pl.ds(pl.multiple_of(1024 * half + 512 * mine + 128 * row, 128), 128)
+            far = pl.ds(pl.multiple_of(512 * half + 128 * row, 128), 128)
+            value = product(branch_ref[:, near], cot_ref[...])
+            value = value + product(far_branch[:, far], far_cot[...])
+            store(row, half, pl.ds(2304, 1024), value)
+
+    begin(2, 0)
+    normed_in.wait_recv()
+    strip_in.wait_recv()
+    for part in range(2):
+        pg_in[part].wait_recv()
+        for half in range(2):
+
+            @pl.loop(0, 4)
+            def _(row):
+                rows = pl.ds(pl.multiple_of(512 * half + 128 * row, 128), 128)
+                near = pl.ds(pl.multiple_of(2304 * part + 1152 * mine, 128), 1152)
+                value = product(normed_ref[:, rows], pg_ref[:, near])
+                value = value + product(
+                    far_normed[:, rows], far_pg[:, 1152 * part : 1152 * part + 1152]
+                )
+                store(row, half, pl.ds(1152 * part, 1152), value)
+                if part == 1:
+                    small = strip_ref[rows, :].astype(jnp.float32) + far_strip[rows, :].astype(
+                        jnp.float32
+                    )
+                    tail = value[:, 1024:] + small * mine.astype(jnp.float32)
+                    store(row, half, pl.ds(2304 - 128, 128), tail)
+
+        begin(part, 0)
+
+    turn = (2, 0, 1)
+    for stage in range(3):
+        for part in turn:
+            relay(part, stage)
+        for part in turn:
+            settle(part, stage)
+            if stage < 2:
+                begin(part, stage + 1)
+
+    out_sizes = {"x": 4, "y": 4, "z": 2}
+    place_out = {"x": here["x"], "y": here["y"], "z": lax.rem(here["z"], 2)}
+
+    def gather_axes(part, stage):
+        order = PARTS[part][:3][::-1]
+        axes = {}
+        for name in order[stage + 1 :]:
+            axes[name] = place_out[name]
+        free = [name for name in ("x", "y", "z") if name in order[:stage]]
+        for name in free:
+            axes[name] = slice(None)
+        return order[stage], axes, free
+
+    to_twin = []
+
+    def share(part, stage, axes):
+        if stage == 2:
+            here_view = view(out_ref, axes, out_cols(part))
+            to_twin.append(copies.start(here_view, here_view, twin))
+
+    def spread(part, stage):
+        axis, axes, free = gather_axes(part, stage)
+        cols = out_cols(part)
+        if axis == "z":
+            low_z = place_out["z"]
+            beside = device_at(dict(here, z=here["z"] + 1 - 2 * low_z))
+            piece = view(out_ref, dict(axes, z=low_z), cols)
+            live["g", part, stage] = (copies.start(piece, piece, beside),)
+            share(part, stage, dict(axes, z=low_z))
+            return
+        ahead, behind = device_at(moved(here, axis, 1)), device_at(moved(here, axis, -1))
+        piece = view(out_ref, dict(axes, **{axis: here[axis]}), cols)
+        up = copies.start(piece, piece, ahead)
+        down = copies.start(piece, piece, behind)
+        live["g", part, stage] = (up, down)
+        share(part, stage, dict(axes, **{axis: here[axis]}))
+
+    def forward(part, stage):
+        axis, axes, free = gather_axes(part, stage)
+        cols = out_cols(part)
+        started = live["g", part, stage]
+        if axis == "z":
+            started[0].wait_recv()
+            live["h", part, stage] = ()
+            share(part, stage, dict(axes, z=1 - place_out["z"]))
+            return
+        ahead, behind = device_at(moved(here, axis, 1)), device_at(moved(here, axis, -1))
+        before = dict(axes, **{axis: lax.rem(here[axis] + 3, 4)})
+        after = dict(axes, **{axis: lax.rem(here[axis] + 1, 4)})
+        started[0].wait_recv()
+        first, _ = halves(before, free, out_sizes)
+        piece = view(out_ref, first, cols)
+        more = [copies.start(piece, piece, ahead)]
+        share(part, stage, before)
+        started[1].wait_recv()
+        if free:
+            _, second = halves(after, free, out_sizes)
+            piece = view(out_ref, second, cols)
+            more.append(copies.start(piece, piece, behind))
+        share(part, stage, after)
+        live["h", part, stage] = tuple(more)
+
+    def complete(part, stage):
+        axis, axes, free = gather_axes(part, stage)
+        for copy in live["h", part, stage]:
+            copy.wait_recv()
+        if axis != "z":
+            share(part, stage, dict(axes, **{axis: lax.rem(here[axis] + 2, 4)}))
+
+    for stage in range(3):
+        for part in turn:
+            spread(part, stage)
+        for part in turn:
+            forward(part, stage)
+        for part in turn:
+            complete(part, stage)
+    for copy in to_twin:
+        copy.wait_recv()
+    copies.finish()
+
+
+def reduce_gradients(normed, proj_grad, branch, cotangent, strip):
+    bf16 = jnp.bfloat16
+    vmem = lambda *shape: pltpu.VMEM(shape, bf16)
+    widths = [part[4] for part in PARTS]
+    scratch = [
+        vmem(256, 1024),
+        vmem(256, 2304),
+        vmem(256, 1024),
+        vmem(256, 1024),
+        vmem(1024, 128),
+        vmem(4, 4, 4, 16, OWN_COLS),
+    ]
+    scratch += [vmem(2, 2, 4, 16, width) for width in widths]
+    scratch += [vmem(2, 4, 4, 16, width) for width in widths]
+    scratch += [vmem(2, 2, 16, width) for width in widths]
+    scratch += [vmem(2, 4, 16, width) for width in widths]
+    scratch += [vmem(3, 16, width) for width in widths]
+    scratch += [pltpu.SemaphoreType.DMA((N_SEMS,)), pltpu.SemaphoreType.DMA((N_SEMS,))]
+    out = pl.pallas_call(
+        reduce_kernel,
+        out_shape=jax.ShapeDtypeStruct((4, 4, 2, 16, ALL_COLS), bf16),
+        in_specs=[pl.BlockSpec(memory_space=pltpu.VMEM)] * 5,
+        out_specs=pl.BlockSpec(memory_space=pltpu.VMEM),
+        scratch_shapes=scratch,
+        compiler_params=pltpu.CompilerParams(
+            collective_id=0, has_side_effects=True, vmem_limit_bytes=56 * 1024 * 1024
+        ),
+        name="reduce_gradients",
+    )(normed, proj_grad, branch, cotangent, strip)
+    return out.reshape(512, ALL_COLS)
 
 
 def on_device(
@@ -218,14 +627,7 @@
     mixed = (inputs + jnp.dot(branch_low, full_out, preferred_element_type=jnp.float32)).astype(
         jnp.bfloat16
     )
-    again = (
-        lax.all_gather(w_in, "grp", axis=0, tiled=True),
-        lax.all_gather(w_out, "grp", axis=0, tiled=True),
-    )
-    back_in = again[0]
-    back_out = again[1]
-    out_grad = jnp.dot(branch_low.T, cotangent, preferred_element_type=jnp.float32)
-    branch_grad = jnp.dot(cotangent, back_out.T, preferred_element_type=jnp.float32)
+    branch_grad = jnp.dot(cotangent, full_out.T, preferred_element_type=jnp.float32)
     ssd_grad, head_gate_grad, gate_in_grad, skip_grad, ggain_grad = gate_pull(branch_grad)
     ssd_grad_blocks = ssd_grad.reshape(blocks, width, HEADS, HEAD_DIM)
     local_grad = jnp.einsum(
@@ -274,34 +676,50 @@
     returned = from_behind(ext_grad[:rim], "grp", -1)
     conv_in_grad = ext_grad[rim:] + jnp.pad(returned, ((count - rim, 0), (0, 0)))
     proj_grad = jnp.concatenate([gate_in_grad, conv_in_grad, raw_grad], axis=1).astype(jnp.bfloat16)
-    in_grad = jnp.dot(normed_low.T, proj_grad, preferred_element_type=jnp.float32)
-    normed_grad = jnp.dot(proj_grad, back_in.T, preferred_element_type=jnp.float32)
+    normed_grad = jnp.dot(proj_grad, full_in.T, preferred_element_type=jnp.float32)
     branch_inputs, igain_grad = pre_pull(normed_grad)
     input_grad = cotangent.astype(jnp.float32) + branch_inputs
+    owned = []
+    for half in range(2):
+        cut = lambda value: lax.slice_in_dim(
+            value, half * (value.shape[-1] // 2), (half + 1) * (value.shape[-1] // 2), axis=-1
+        ).reshape(-1)
+        small = jnp.concatenate(
+            [
+                cut(igain_grad),
+                cut(conv_w_grad),
+                cut(conv_b_grad),
+                cut(bias_grad),
+                cut(alog_grad),
+                cut(skip_grad),
+                cut(ggain_grad),
+            ]
+        )
+        owned.append(jnp.pad(small, (0, 512 * LANES - small.shape[0])).reshape(512, LANES))
+    strip = jnp.concatenate(owned, axis=0).astype(jnp.bfloat16)
+    padded = jnp.pad(proj_grad, ((0, 0), (0, W_IN_COLS - proj_grad.shape[1])))
+    reduced = reduce_gradients(normed_low, padded, branch_low, cotangent, strip)
+    w_in_sum = reduced[:, : proj_grad.shape[1]].astype(jnp.float32)
+    w_out_sum = jnp.concatenate(
+        [reduced[:, W_IN_COLS : W_IN_COLS + 1024], reduced[:, W_IN_COLS + 1024 :]], axis=0
+    ).astype(jnp.float32)
+    flat = reduced[:64, W_IN_COLS - LANES : W_IN_COLS].astype(jnp.float32).reshape(-1)
+    sizes = (512, 4608, 1152, 16, 16, 16, 1024)
+    pieces = []
+    start = 0
+    for size in sizes:
+        pieces.append(flat[start : start + size])
+        start += size
     summed = (
-        lax.psum_scatter(igain_grad, "grp", scatter_dimension=0, tiled=True),
-        lax.psum_scatter(in_grad, "grp", scatter_dimension=0, tiled=True),
-        lax.psum_scatter(conv_w_grad, "grp", scatter_dimension=1, tiled=True),
-        lax.psum_scatter(conv_b_grad, "grp", scatter_dimension=0, tiled=True),
-        lax.psum_scatter(bias_grad, "grp", scatter_dimension=0, tiled=True),
-        lax.psum_scatter(alog_grad, "grp", scatter_dimension=0, tiled=True),
-        lax.psum_scatter(skip_grad, "grp", scatter_dimension=0, tiled=True),
-        lax.psum_scatter(ggain_grad, "grp", scatter_dimension=0, tiled=True),
-        lax.psum_scatter(out_grad, "grp", scatter_dimension=0, tiled=True),
-    )
-    summed = lax.psum(
-        (
-            summed[0],
-            summed[1],
-            summed[2],
-            summed[3],
-            summed[4],
-            summed[5],
-            summed[6],
-            summed[7],
-            summed[8],
-        ),
-        "rep",
+        pieces[0],
+        w_in_sum,
+        pieces[1].reshape(4, 1152),
+        pieces[2],
+        pieces[3],
+        pieces[4],
+        pieces[5],
+        pieces[6],
+        w_out_sum,
     )
     return (
         mixed,

time: 1260 us -> 529 us (0.42)
  waiting for transfers between devices: 706 us -> 150 us
  blocking collectives: 316 us -> 34.6 us
  Pallas kernels: 0 us -> 92.5 us
  local copies, waits for them, and re-layouts: 40 us -> 62.4 us
    psum x1 -> x0, waiting for transfers between devices: 311 us -> none  [on_device(): lax.psum((summed[0], summed[1], summed[2], summed[3], summed[4], summed[5...]
    psum x1 -> x0, blocking collectives: 274 us -> none  [on_device(): lax.psum((summed[0], summed[1], summed[2], summed[3], summed[4], summed[5...]
    reduce_scatter x2 -> x0, waiting for transfers between devices: 243 us -> none  [the longest x1 207 us: on_device(): lax.psum_scatter(in_grad, 'grp', scatter_dimension=0, tiled=True)]
    pallas_call x0 -> x1, Pallas kernels: none -> 92.5 us  [reduce_gradients(): pl.pallas_call(reduce_kernel, out_shape=jax.ShapeDtypeStruct((4, 4, 2, 16...]
    all_gather x1, waiting for transfers between devices: 20.1 us -> 3.62 us  [entering(): everything = jax.tree.map(lambda part: lax.all_gather(part, axis), shard)]
    dot_general x4 -> x2, matrix products: 27.1 us -> 12.1 us  [the longest x1 7.25 us: on_device(): jnp.dot(proj_grad, full_in.T, preferred_element_type=jnp.float32)]
    all_gather x1, waiting for transfers between devices: 0.01 us -> 14.1 us  [prefix(): lax.all_gather(part.astype(kind), axis)]
    unnamed x228 -> x178, local copies, waits for them, and re-layouts: 25.4 us -> 13.6 us
  transfers between devices with their start and end apart: 11 -> 7, of which waited for: 7 -> 4; matrix products, arithmetic and copies ran while one was open for 11% -> 13% of each run, Pallas kernels for 0% -> 0%
where the time goes in v1:
time: 529 us; the launch traced here: 520 us
  waiting for transfers between devices  150 us (28%)
  Pallas kernels  92.5 us (17%)
  matrix products  92.4 us (17%)
  local copies, waits for them, and re-layouts  62.4 us (12%)
  other arithmetic  61.9 us (12%)
  blocking collectives  34.6 us (7%)
  between operations  16 us (3%)
  starting transfers between devices  9.63 us (2%)
    pallas_call x1, Pallas kernels, reduce_gradients(): pl.pallas_call(reduce_kernel, out_shape=jax.ShapeDtypeStruct((4, 4, 2, 16...  92.5 us
    all_gather x1, waiting for transfers between devices, on_device(): lax.all_gather(w_in, 'grp', axis=0, tiled=True)  88.2 us
    all_gather x1, waiting for transfers between devices, on_device(): lax.all_gather(w_out, 'grp', axis=0, tiled=True)  42.9 us
    dot_general x3, matrix products, ssd_block(): output = jnp.einsum('tsh,shd->thd', weights, head_in, precision=HIGHEST)  36.6 us
    all_gather x1, waiting for transfers between devices, prefix(): lax.all_gather(part.astype(kind), axis)  14.1 us
    unnamed x178, local copies, waits for them, and re-layouts  13.6 us
    dot_general x3, matrix products, ssd_block(): jnp.einsum('shd,sn->hdn', head_in * (step_size * tail)[:, :, None], b_mat...  11.9 us
  transfers between devices with their start and end apart: 7, of which 4 were waited for; matrix products, arithmetic and copies ran while one was open for 13% of the time, Pallas kernels for 0%

profile of v1, /device:TPU:1, one launch (start us, length us, event | category | flops | bytes accessed | tf_op | source)
XLA Modules:
  0.0 519.8 jit_solution(8821149392783196361)
XLA Ops:
  8.1 6.3 %collective-permute-start.1 = (f32[3]{0:T(128)S(1)}, f32[3]{0:T(128)S(1)}, u32[]{:S(2)}, u32[]{:S(2)}) collective-permute-start(f32[3]{0:T(128)S(1)} %slice_convert_fusion.2), channel_id=1, source_target_pairs={{0,1},{2,3},{4,5},{6,7},{8,9},{10,11},{12,13},{14,15},{16,17},{18,... | collective-permute-start | bytes 44 | tf_op jit(solution)/shard_map/ppermute | solution.py:23
  15.1 4.7 all-gather.3
  19.7 4.7 all_gather.48
  24.5 4.7 all-gather.2
  31.9 6.2 %all-reduce.20 = (bf16[32]{0:T(256)(128)(2,1)}, bf16[32]{0:T(256)(128)(2,1)S(1)}, bf16[32]{0:T(256)(128)(2,1)S(1)}) all-reduce(bf16[32]{0:T(256)(128)(2,1)S(1)} %dynamic-update-slice.2, bf16[32]{0:T(256)(128)(2,1)S(1)} %dynamic-update-slice, bf16[32]{0:T(256)(128)(2,1)S(1)} %dynamic-update-slice.1), channel_id=1, replica_groups=mesh['rep'=64,'grp'=2] {'grp'}, use_global_device_ids=true, to_apply=%add.19 | all-reduce | flops 96 | bytes 384
  40.2 1.9 compare_convert_fusion.4
  42.1 88.2 %all-gather.11.cloned.1.call-done = bf16[1024,4384]{0,1:T(8,128)(2,1)} async-done(((bf16[512,4384]{0,1:T(8,128)(2,1)}), bf16[1024,4384]{0,1:T(8,128)(2,1)}) %all-gather.11.cloned.1.call-update) | async-done | bytes 8978448 | tf_op jit(solution)/shard_map/all_gather | solution.py:549
  130.3 6.2 %fusion.108 = f32[256,4384]{1,0:T(8,128)S(1)} fusion(bf16[256,1024]{1,0:T(8,128)(2,1)S(1)} %fusion.55.normed_ref, bf16[1024,4384]{0,1:T(8,128)(2,1)} %all-gather.11.cloned.1.call-done), kind=kOutput, calls=%fused_computation.201 | convolution fusion | flops 2298478592 | bytes 13991936 | tf_op jit(solution)/shard_map/dot_general | solution.py:572
  140.5 3.3 slice.275
  143.9 7.3 %fusion.29 = (f32[256,2304]{1,0:T(8,128)S(1)}, f32[256,2304]{1,0:T(8,128)}) fusion(f32[256,2304]{1,0:T(8,128)} %slice.275, f32[2304]{0:T(1024)S(1)} %get-tuple-element.434, f32[256]{0:T(256)S(1)} %copy-done.44, f32[3,2304]{1,0:T(4,128)S(1)} %collective-permute-done, f32[2304]{0:T(1024)S(1)} %get-tuple-element.435, f32[256]{0:T(256)S(1)} %copy-done.46, ...), kind=kLoop, calls=%fused_computation.50 | loop fusion | flops 10616832 | bytes 7154688 | tf_op jit(solution)/shard_map/jvp(jit(silu))/mul | solution.py:79
  153.0 2.9 copy.122
  155.9 4.4 fusion.43
  161.3 4.7 all_gather.57
  166.1 4.6 all-gather.5
  172.5 3.0 copy.134
  175.5 5.0 all-gather.4
  181.8 12.3 %fusion.8 = f32[32,64,256]{2,1,0:T(8,128)} fusion(f32[256,32,64]{0,2,1:T(8,128)} %bitcast.158, f32[256,32]{0,1:T(8,128)S(1)} %copy.129, f32[256,256]{1,0:T(8,128)S(1)} %fusion.82, f32[256,32]{0,1:T(8,128)S(1)} %copy.127, pred[256,256]{1,0:T(8,128)(4,1)S(1)} %fusion.66), kind=kOutput, calls=%fused_computation.16 | convolution fusion | flops 1621098496 | bytes 4587520 | tf_op jit(solution)/shard_map/while/body/eval_jaxpr/tsh,shd->thd/dot_general | solution.py:100
  194.1 3.6 all-gather.15.cloned.1.call-done
  197.7 3.0 while.20
  200.7 2.9 fusion.76
  203.6 4.4 fusion.33
  208.1 3.2 copy.132
  211.2 5.5 %multiply_reduce_fusion.10 = (f32[256]{0:T(256)S(1)}, f32[256,2048]{1,0:T(8,128)}) fusion(f32[256,4384]{1,0:T(8,128)} %copy-done.9, f32[256,2048]{1,0:T(8,128)} %copy.132, f32[256,2304]{1,0:T(8,128)} %copy-done, f32[2048]{0:T(1024)S(1)} %mul.683), kind=kLoop, calls=%fused_computation.72 | loop fusion | flops 4718336 | bytes 8397824 | tf_op jit(solution)/shard_map/jvp()/reduce_sum | solution.py:119
  216.7 42.9 %all-gather.13.cloned.1.call-done = bf16[2048,1024]{1,0:T(8,128)(2,1)} async-done(((bf16[1024,1024]{1,0:T(8,128)(2,1)}), bf16[2048,1024]{1,0:T(8,128)(2,1)}) %all-gather.13.cloned.1.call-update) | async-done | bytes 4194320 | tf_op jit(solution)/shard_map/all_gather | solution.py:557
  259.6 4.8 multiply_reduce_fusion.5
  265.0 4.6 multiply_reduce_fusion.6
  269.6 3.4 copy.136
  273.0 15.5 %fusion.11 = (f32[256,32]{0,1:T(8,128)S(1)}, f32[256,32]{0,1:T(8,128)S(1)}, f32[256,32]{0,1:T(8,128)S(1)}, f32[256,256]{1,0:T(8,128)}) fusion(f32[256,32]{0,1:T(8,128)S(1)} %copy.129, f32[256,256]{1,0:T(8,128)S(1)} %fusion.82, f32[256,32]{0,1:T(8,128)S(1)} %copy.127, pred[256,256]{1,0:T(8,128)(4,1)S(1)} %fusion.66, f32[32,64,256]{2,1,0:T(8,128)} %bitcast.164, ...), kind=kOutput, calls=%fused_computation.19 | convolution fusion | flops 1641979904 | bytes 4947968 | tf_op jit(solution)/shard_map/while/body/eval_jaxpr/transpose(jvp(tsh,shd->thd))/dot_general | solution.py:100
  290.0 4.2 fusion.47
  294.2 2.7 multiply_reduce_fusion.7
  300.3 4.7 fusion.46
  305.0 14.1 %all-gather.17.cloned.1.call-done = bf16[64,64,128]{2,1,0:T(8,128)(2,1)} async-done(((bf16[32,64,128]{2,1,0:T(8,128)(2,1)}), bf16[64,64,128]{2,1,0:T(8,128)(2,1)}) %all-gather.17.cloned.1.call-update) | async-done | bytes 1048592 | tf_op jit(solution)/shard_map/all_gather | solution.py:46
  319.0 2.8 while.21
  323.4 3.4 multiply_reduce_fusion.8
  326.9 4.1 fusion.52
  331.0 8.8 %bitcast_add_fusion.1 = f32[256,32,64]{0,2,1:T(8,128)} fusion(f32[256,32,64]{0,2,1:T(8,128)S(1)} %get-tuple-element.502, f32[32,64,256]{2,1,0:T(8,128)S(1)} %bitcast.166, f32[256,32]{0,1:T(8,128)S(1)} %copy.129, f32[256,256]{1,0:T(8,128)S(1)} %fusion.82, f32[256,32]{0,1:T(8,128)S(1)} %copy.127, pred[256,256]{1,0:T(8,128)(4,1)S(1)} %fusion.66, ...), kind=kOutput, calls=%fused_computation.60 | convolution fusion | flops 1622147072 | bytes 6717440 | tf_op jit(solution)/shard_map/while/body/eval_jaxpr/transpose(jvp(tsh,shd->thd))/dot_general | solution.py:100
  339.8 3.1 copy.137
  342.9 4.9 fusion.104
  347.8 3.2 copy.135
  351.1 5.2 convolution_bitcast_fusion
  359.4 4.9 multiply_reduce_fusion.3
  367.2 2.5 reduce-window.24
  383.9 7.2 %fusion.56 = (bf16[1024]{0:T(1024)(128)(2,1)S(1)}, f32[256]{0:T(256)S(1)}, f32[256,1024]{1,0:T(8,128)}) fusion(bf16[256,1024]{1,0:T(8,128)(2,1)S(1)} %copy-done.15, f32[256]{0:T(256)S(1)} %copy-done.52, f32[1024]{0:T(1024)S(1)} %bitcast.178, bf16[1024,4384]{0,1:T(8,128)(2,1)} %all-gather.11.cloned.1.call-done, bf16[256,32]{1,0:T(8,128)(2,1)S(1)} %copy-done.24, ...), kind=kOutput, calls=%fused_computation.97 | convolution fusion | flops 2307046144 | bytes 12804096 | tf_op jit(solution)/shard_map/dot_general | solution.py:679
  393.9 92.5 %reduce_gradients.1 = bf16[4,4,2,16,6656]{4,3,2,1,0:T(8,128)(2,1)} custom-call(bf16[256,1024]{1,0:T(8,128)(2,1)} %copy-done.19, bf16[256,4608]{1,0:T(8,128)(2,1)} %pad.68.pg_ref, bf16[256,2048]{1,0:T(8,128)(2,1)} %get-tuple-element.480.branch_ref, bf16[256,1024]{1,0:T(8,128)(2,1)} %cot_ref.1, bf16[1024,128]{1,0:T(8,128)(2,1)} %pad_maximum_fusion.2.strip_ref), custom_call_target="tpu_custom_call" | custom-call | tf_op jit(solution)/shard_map/reduce_gradients/pallas_call | solution.py:520
  487.1 6.5 %slice_convert_fusion = f32[512,4384]{1,0:T(8,128)} fusion(bf16[512,6656]{1,0:T(8,128)(2,1)} %bitcast.162), kind=kLoop, calls=%fused_computation.17 | loop fusion | flops 2244608 | bytes 13467648 | tf_op jit(solution)/shard_map/convert_element_type | solution.py:702
  497.7 9.5 %copy.147 = f32[512,4384]{0,1:T(8,128)} copy(f32[512,4384]{1,0:T(8,128)} %slice_convert_fusion) | data formatting | bytes 17956864
  507.9 2.5 fusion.57
  510.4 2.5 maximum_convert_fusion
  (301 shorter events, 56.2 us)
Async XLA Ops:
  7.2 22.7 %copy-start.82 = (u32[128]{0:T(128)S(1)}, u32[128]{0:T(128)}, u32[]{:S(2)}) copy-start(u32[128]{0:T(128)} %constant.187) | copy-start | bytes 1540
  7.2 7.8 %copy-start.70 = (bf16[512]{0:T(512)(128)(2,1)S(1)}, bf16[512]{0:T(512)(128)(2,1)}, u32[]{:S(2)}) copy-start(bf16[512]{0:T(512)(128)(2,1)} %param.18) | copy-start | bytes 3076
  7.2 12.5 %copy-start.56 = (bf16[4,1152]{1,0:T(4,128)(2,1)S(1)}, bf16[4,1152]{1,0:T(4,128)(2,1)}, u32[]{:S(2)}) copy-start(bf16[4,1152]{1,0:T(4,128)(2,1)} %param.20) | copy-start | bytes 27652
  7.2 17.3 %copy-start.63 = (bf16[1152]{0:T(1024)(128)(2,1)S(1)}, bf16[1152]{0:T(1024)(128)(2,1)}, u32[]{:S(2)}) copy-start(bf16[1152]{0:T(1024)(128)(2,1)} %param.21) | copy-start | bytes 6916
  7.2 23.9 %copy-start.77 = (bf16[16]{0:T(256)(128)(2,1)S(1)}, bf16[16]{0:T(256)(128)(2,1)}, u32[]{:S(2)}) copy-start(bf16[16]{0:T(256)(128)(2,1)} %param.24) | copy-start | bytes 100
  7.2 24.1 %copy-start.78 = (bf16[16]{0:T(256)(128)(2,1)S(1)}, bf16[16]{0:T(256)(128)(2,1)}, u32[]{:S(2)}) copy-start(bf16[16]{0:T(256)(128)(2,1)} %param.22) | copy-start | bytes 100
  7.3 24.4 %copy-start.79 = (bf16[16]{0:T(256)(128)(2,1)S(1)}, bf16[16]{0:T(256)(128)(2,1)}, u32[]{:S(2)}) copy-start(bf16[16]{0:T(256)(128)(2,1)} %param.23) | copy-start | bytes 100
  7.3 31.5 %copy-start.14 = (bf16[256,1024]{1,0:T(8,128)(2,1)S(1)}, bf16[256,1024]{1,0:T(8,128)(2,1)}, u32[]{:S(2)}) copy-start(bf16[256,1024]{1,0:T(8,128)(2,1)} %param.16) | copy-start | bytes 1572868
  7.3 123.0 %all-gather.11.cloned.1.call-start = ((), (), s32[]{:S(2)}) async-start(), calls=%async_computation | async-start | bytes 13467648 | tf_op jit(solution)/shard_map/all_gather | solution.py:549
  8.0 189.7 %all-gather.15.cloned.1.call-start = ((), (), s32[]{:S(2)}) async-start(), calls=%async_computation.2 | async-start | bytes 3145728 | tf_op jit(solution)/shard_map/all_gather | solution.py:28
  8.1 31.1 %collective-permute-start.1 = (f32[3]{0:T(128)S(1)}, f32[3]{0:T(128)S(1)}, u32[]{:S(2)}, u32[]{:S(2)}) collective-permute-start(f32[3]{0:T(128)S(1)} %slice_convert_fusion.2), channel_id=1, source_target_pairs={{0,1},{2,3},{4,5},{6,7},{8,9},{10,11},{12,13},{14,15},{16,17},{18,... | collective-permute-start | bytes 44 | tf_op jit(solution)/shard_map/ppermute | solution.py:23
  38.1 100.0 %copy-start.64 = (f32[32]{0:T(128)}, f32[32]{0:T(128)S(1)}, u32[]{:S(2)}) copy-start(f32[32]{0:T(128)S(1)} %convert_element_type.128) | copy-start | bytes 388
  38.8 105.1 %copy-start.28 = (f32[2304]{0:T(1024)}, f32[2304]{0:T(1024)S(1)}, u32[]{:S(2)}) copy-start(f32[2304]{0:T(1024)S(1)} %get-tuple-element.434) | copy-start | bytes 27652
  38.8 105.1 %copy-start.30 = (f32[2304]{0:T(1024)}, f32[2304]{0:T(1024)S(1)}, u32[]{:S(2)}) copy-start(f32[2304]{0:T(1024)S(1)} %get-tuple-element.435) | copy-start | bytes 27652
  39.0 99.1 %copy-start.65 = (f32[32]{0:T(128)}, f32[32]{0:T(128)S(1)}, u32[]{:S(2)}) copy-start(f32[32]{0:T(128)S(1)} %fusion.92) | copy-start | bytes 388
  39.2 97.2 %copy-start.19 = (bf16[256,1024]{1,0:T(8,128)(2,1)}, bf16[256,1024]{1,0:T(8,128)(2,1)S(1)}, u32[]{:S(2)}) copy-start(bf16[256,1024]{1,0:T(8,128)(2,1)S(1)} %fusion.55.normed_ref) | copy-start | bytes 1572868
  42.1 97.7 %copy-start.40 = (f32[256]{0:T(256)}, f32[256]{0:T(256)S(1)}, u32[]{:S(2)}) copy-start(f32[256]{0:T(256)S(1)} %get-tuple-element.497) | copy-start | bytes 3076
  42.1 97.7 %copy-start.57 = (f32[256]{0:T(256)}, f32[256]{0:T(256)S(1)}, u32[]{:S(2)}) copy-start(f32[256]{0:T(256)S(1)} %get-tuple-element.496) | copy-start | bytes 3076
  136.5 7.3 %collective-permute-start = (f32[3,2304]{1,0:T(4,128)S(1)}, f32[3,2304]{1,0:T(4,128)S(1)}, u32[]{:S(2)}, u32[]{:S(2)}) collective-permute-start(f32[3,2304]{1,0:T(4,128)S(1)} %slice.274), channel_id=1, source_target_pairs={{0,1},{2,3},{4,5},{6,7},{8,9},{10,11},{12,13},{14,15},{16,17},{18,... | collective-permute-start | bytes 82952 | tf_op jit(solution)/shard_map/ppermute | solution.py:23
  139.8 31.0 %copy-start.12 = (f32[32,2,128]{0,2,1:T(8,128)}, f32[32,2,128]{0,2,1:T(8,128)S(1)}, u32[]{:S(2)}) copy-start(f32[32,2,128]{0,2,1:T(8,128)S(1)} %copy.126) | copy-start | bytes 98308
  143.8 7.4 %copy-start.25 = (f32[3,2304]{1,0:T(4,128)}, f32[3,2304]{1,0:T(4,128)S(1)}, u32[]{:S(2)}) copy-start(f32[3,2304]{1,0:T(4,128)S(1)} %collective-permute-done) | copy-start | bytes 82948
  151.2 4.7 copy-start
  160.3 5.7 %copy-start.49 = (s32[256]{0:T(256)S(1)}, s32[256]{0:T(256)}, u32[]{:S(2)}) copy-start(s32[256]{0:T(256)} %param.17) | copy-start | bytes 3076
  160.3 99.2 %all-gather.13.cloned.1.call-start = ((), (), s32[]{:S(2)}) async-start(), calls=%async_computation.1 | async-start | bytes 6291456 | tf_op jit(solution)/shard_map/all_gather | solution.py:557
  161.1 157.9 %all-gather.17.cloned.1.call-start = ((), (), s32[]{:S(2)}) async-start(), calls=%async_computation.3 | async-start | bytes 1572864 | tf_op jit(solution)/shard_map/all_gather | solution.py:46
  203.6 4.4 copy-start.4
  259.6 5.5 %copy-start.1 = (f32[256,2304]{1,0:T(8,128)S(1)}, f32[256,2304]{1,0:T(8,128)}, u32[]{:S(2)}) copy-start(f32[256,2304]{1,0:T(8,128)} %copy-done) | copy-start | bytes 7077892
  259.6 5.5 %copy-start.6 = (f32[256,2048]{1,0:T(8,128)S(1)}, f32[256,2048]{1,0:T(8,128)}, u32[]{:S(2)}) copy-start(f32[256,2048]{1,0:T(8,128)} %copy.132) | copy-start | bytes 6291460
  259.6 5.5 %copy-start.7 = (f32[256,2048]{1,0:T(8,128)S(1)}, f32[256,2048]{1,0:T(8,128)}, u32[]{:S(2)}) copy-start(f32[256,2048]{1,0:T(8,128)} %get-tuple-element.466) | copy-start | bytes 6291460
  347.8 11.5 %copy-start.10 = (f32[256,2304]{1,0:T(8,128)S(1)}, f32[256,2304]{1,0:T(8,128)}, u32[]{:S(2)}) copy-start(f32[256,2304]{1,0:T(8,128)} %get-tuple-element.470) | copy-start | bytes 7077892
  351.0 8.3 %copy-start.3 = (f32[256,2304]{1,0:T(8,128)S(1)}, f32[256,2304]{1,0:T(8,128)}, u32[]{:S(2)}) copy-start(f32[256,2304]{1,0:T(8,128)} %slice.275) | copy-start | bytes 7077892
  351.1 8.3 %copy-start.11 = (f32[256,2048]{1,0:T(8,128)S(1)}, f32[256,2048]{1,0:T(8,128)}, u32[]{:S(2)}) copy-start(f32[256,2048]{1,0:T(8,128)} %get-tuple-element.482) | copy-start | bytes 6291460
  351.1 8.3 %copy-start.26 = (f32[3,2304]{1,0:T(4,128)S(1)}, f32[3,2304]{1,0:T(4,128)}, u32[]{:S(2)}) copy-start(f32[3,2304]{1,0:T(4,128)} %copy-done.25) | copy-start | bytes 82948
  351.1 8.3 %copy-start.43 = (f32[256]{0:T(256)S(1)}, f32[256]{0:T(256)}, u32[]{:S(2)}) copy-start(f32[256]{0:T(256)} %get-tuple-element.493) | copy-start | bytes 3076
  351.1 8.2 %copy-start.45 = (f32[256]{0:T(256)S(1)}, f32[256]{0:T(256)}, u32[]{:S(2)}) copy-start(f32[256]{0:T(256)} %get-tuple-element.494) | copy-start | bytes 3076
  351.1 8.2 %copy-start.47 = (f32[256]{0:T(256)S(1)}, f32[256]{0:T(256)}, u32[]{:S(2)}) copy-start(f32[256]{0:T(256)} %get-tuple-element.495) | copy-start | bytes 3076
  359.4 4.9 copy-start.29
  359.4 4.9 copy-start.31
  359.4 4.9 copy-start.33
  365.9 6.4 %copy-start.37 = (f32[2304]{0:T(1024)S(1)}, f32[2304]{0:T(1024)}, u32[]{:S(2)}) copy-start(f32[2304]{0:T(1024)} %get-tuple-element.425) | copy-start | bytes 27652
  365.9 6.4 %copy-start.36 = (f32[2304]{0:T(1024)S(1)}, f32[2304]{0:T(1024)}, u32[]{:S(2)}) copy-start(f32[2304]{0:T(1024)} %get-tuple-element.424) | copy-start | bytes 27652
  365.9 6.4 %copy-start.35 = (f32[2304]{0:T(1024)S(1)}, f32[2304]{0:T(1024)}, u32[]{:S(2)}) copy-start(f32[2304]{0:T(1024)} %get-tuple-element.430) | copy-start | bytes 27652
  366.0 7.1 %copy-start.20 = (f32[256,32]{1,0:T(8,128)S(1)}, f32[256,32]{1,0:T(8,128)}, u32[]{:S(2)}) copy-start(f32[256,32]{1,0:T(8,128)} %copy.139) | copy-start | bytes 98308
  370.0 11.8 %collective-permute-start.2 = (f32[3,2304]{1,0:T(4,128)}, f32[3,2304]{1,0:T(4,128)}, u32[]{:S(2)}, u32[]{:S(2)}) collective-permute-start(f32[3,2304]{1,0:T(4,128)} %pad_add_fusion.1), channel_id=1, source_target_pairs={{1,0},{3,2},{5,4},{7,6},{9,8},{11,10},{13,12},{15,14},{17,16},{19,... | collective-permute-start | bytes 82952 | tf_op jit(solution)/shard_map/ppermute | solution.py:23
  374.7 8.2 %copy-start.17 = (bf16[256,2048]{1,0:T(8,128)(2,1)S(1)}, bf16[256,2048]{1,0:T(8,128)(2,1)}, u32[]{:S(2)}) copy-start(bf16[256,2048]{1,0:T(8,128)(2,1)} %get-tuple-element.471) | copy-start | bytes 3145732
  374.7 8.2 %copy-start.24 = (bf16[256,32]{1,0:T(8,128)(2,1)S(1)}, bf16[256,32]{1,0:T(8,128)(2,1)}, u32[]{:S(2)}) copy-start(bf16[256,32]{1,0:T(8,128)(2,1)} %get-tuple-element.463) | copy-start | bytes 49156
  497.7 10.1 %copy-start.16 = (bf16[256,1024]{1,0:T(8,128)(2,1)S(1)}, bf16[256,1024]{1,0:T(8,128)(2,1)}, u32[]{:S(2)}) copy-start(bf16[256,1024]{1,0:T(8,128)(2,1)} %cot_ref.1) | copy-start | bytes 1572868
  497.7 10.1 %copy-start.53 = (f32[256]{0:T(256)S(1)}, f32[256]{0:T(256)}, u32[]{:S(2)}) copy-start(f32[256]{0:T(256)} %copy-done.51) | copy-start | bytes 3076
  (42 other events, 80.2 us)
Sparse Core Ops, SparseCore 0:
  9.8 120.4 all-gather.10
  160.4 37.2 all-gather.14
  199.4 60.1 all-gather.12
  294.3 24.6 all-gather.16

commit v2 on v0

v2 whole, which is shorter than its diff:
```python
import jax
import jax.numpy as jnp
from jax import lax
from jax.experimental import pallas as pl
from jax.experimental.pallas import tpu as pltpu
from jax.sharding import PartitionSpec as P

EPS = 1e-05
SEQ = 512
OWN = 1024
MIX = 1280
HELD = 2432
EXACT = lax.Precision.HIGHEST
FAR = -1e30


def dot(left, right, over=(1, 0), exact=False):
    return lax.dot_general(
        left,
        right,
        (((over[0],), (over[1],)), ((), ())),
        preferred_element_type=jnp.float32,
        precision=EXACT if exact else None,
    )


def split(value, count):
    parts, rest = [], value
    for _ in range(count):
        parts.append(rest.astype(jnp.bfloat16))
        rest = rest - parts[-1].astype(jnp.float32)
    return parts


def pick(left, chosen, count, over=0):
    parts = jnp.concatenate(split(left, count), axis=1)
    return dot(parts, jnp.concatenate([chosen] * count, axis=over), (1, over))


def summed(chosen, right):
    width = right.shape[1]
    total = dot(chosen, jnp.concatenate(split(right, 3), axis=1))
    return total[:, 0:width] + total[:, width : 2 * width] + total[:, 2 * width :]


def near_exact(left, right, over):
    (a, b), (c, d) = split(left, 2), split(right, 2)
    joined = jnp.concatenate([a, a, b], axis=1)
    return dot(joined, jnp.concatenate([c, d, c], axis=over), (1, over))


def iota(shape, axis):
    return lax.broadcasted_iota(jnp.int32, shape, axis)


def turned(value):
    return jnp.transpose(value)


def layer_kernel(
    grp,
    cot_ready,
    exchange,
    send_mixed,
    send_pg,
    proj,
    vec,
    seg,
    tokens,
    cot,
    w_out,
    w_in,
    branch_out,
    pg_out,
    ng_out,
    strip_out,
    vecs_out,
    turned_branch,
    turned_pg,
    act,
    pre,
    same,
    spread,
    run_t,
    scores,
    bias,
    low_x,
    y,
    bg,
    low_dy,
    turned_dy,
    turned_dx,
    d_scores,
    strip,
    stats,
    far_stats,
):
    f32, bf16 = jnp.float32, jnp.bfloat16
    tile = lambda at: pl.ds(pl.multiple_of(128 * at, 128), 128)
    seg_row = seg[0:1, :].astype(f32)
    seg_col = turned(jnp.broadcast_to(seg_row, (128, SEQ)))
    places = iota((SEQ, 128), 0)
    for k in range(1, 4):
        behind = pltpu.roll(seg_col, k, 0)
        same[k - 1] = jnp.where((places >= k) & (behind == seg_col), 1.0, 0.0)
    rows, cols = iota((SEQ, SEQ), 0), iota((SEQ, SEQ), 1)
    seg_wide = jnp.concatenate([seg_col] * 4, axis=1)
    bias[...] = jnp.where((rows >= cols) & (seg_wide == seg_row), 0.0, FAR)

    @pl.loop(0, 10)
    def _(j):
        value = proj[:, pl.ds(pl.multiple_of(1024 + 128 * j, 128), 128)]
        total = vec[4:5, tile(j)] + vec[3:4, tile(j)] * value
        for k in range(1, 4):
            total = total + vec[3 - k : 4 - k, tile(j)] * (pltpu.roll(value, k, 0) * same[k - 1])
        pre[:, tile(j)] = total
        act[:, tile(j)] = total * jax.nn.sigmoid(total)

    heads = 16 * grp
    raw = proj[:, 2304:2432] + vec[6:7, 0:128]
    step = jnp.maximum(raw, 0.0) + jnp.log1p(jnp.exp(-jnp.abs(raw)))
    rate = -jnp.exp(vec[7:8, 0:128])
    down = jnp.where(rows >= cols, 1.0, 0.0).astype(bf16)
    running = summed(down, step * rate)
    run_t[...] = turned(running)
    widen = jnp.where(iota((128, 2048), 0) == heads + iota((128, 2048), 1) // 128, 1.0, 0.0)
    spread[...] = pick(running, widen.astype(bf16), 3)
    expand = jnp.where(iota((128, OWN), 0) == heads + iota((128, OWN), 1) // 64, 1.0, 0.0)
    expand = expand.astype(bf16)
    step_wide = pick(step, expand, 2)
    skip_wide = pick(jnp.broadcast_to(vec[8:9, 0:128], (8, 128)), expand, 2)[0:1]
    low_x[...] = (act[:, 0:OWN] * step_wide).astype(bf16)
    b_mat, c_mat = act[:, 1024:1152], act[:, 1152:1280]
    scores[...] = near_exact(c_mat, b_mat, 1)
    left_lanes = iota((256, 128), 1) < 64

    def decay(head, i, j):
        mine = spread[256 * i : 256 * i + 256, tile(head)]
        theirs = run_t[pl.ds(heads + head, 1), 256 * j : 256 * j + 256]
        mine = jnp.concatenate([mine, mine], axis=1)
        return jnp.exp(mine - theirs + bias[256 * i : 256 * i + 256, 256 * j : 256 * j + 256])

    def block(i, j):
        return (slice(256 * i, 256 * i + 256), slice(256 * j, 256 * j + 256))

    @pl.loop(0, 8)
    def _(p):
        for i in range(2):
            parts = []
            for e in range(2):
                total = None
                for j in range(i + 1):
                    weight = (decay(2 * p + e, i, j) * scores[block(i, j)]).astype(bf16)
                    term = dot(weight, low_x[256 * j : 256 * j + 256, tile(p)])
                    total = term if total is None else total + term
                parts.append(total)
            y[256 * i : 256 * i + 256, tile(p)] = jnp.where(left_lanes, parts[0], parts[1])

    cot_ready()
    bg[...] = dot(cot[...], w_out[...], (1, 1))
    squares = jnp.zeros((SEQ, 128), f32)
    crosses = jnp.zeros((SEQ, 128), f32)
    for j in range(8):
        at = slice(128 * j, 128 * j + 128)
        gate = proj[:, at]
        full = y[:, at] + skip_wide[:, at] * act[:, at]
        gated = full * (gate * jax.nn.sigmoid(gate))
        squares = squares + gated * gated
        crosses = crosses + bg[:, at] * vec[5:6, at] * gated
    ones = jnp.ones((8, 128), f32)
    first = dot(ones, squares, (1, 1), exact=True)
    second = dot(ones, crosses, (1, 1), exact=True)
    stats[...] = jnp.where(iota((8, SEQ), 0) == 0, first, second)
    exchange()
    whole = (stats[...] + far_stats[...]) * (1.0 / 2048)
    root_row = lax.rsqrt(whole[0:1] + EPS)
    cross_row = whole[1:2] * root_row * root_row
    root = turned(jnp.broadcast_to(root_row, (128, SEQ)))
    cross = turned(jnp.broadcast_to(cross_row, (128, SEQ)))

    strip[...] = jnp.zeros((1024, 128), f32)
    skip_sum = []
    for j in range(8):
        at = slice(128 * j, 128 * j + 128)
        gate = proj[:, at]
        sig = jax.nn.sigmoid(gate)
        opened = gate * sig
        full = y[:, at] + skip_wide[:, at] * act[:, at]
        gated = full * opened
        scaled = gated * root
        branch_out[:, at] = (scaled * vec[5:6, at]).astype(bf16)
        back = bg[:, at]
        strip[pl.ds(512 * grp + 49 + j, 1), :] = jnp.sum(back * scaled, axis=0, keepdims=True)
        d_gated = root * (back * vec[5:6, at] - gated * cross)
        d_full = d_gated * opened
        d_gate = d_gated * full * (sig * (1.0 + gate * (1.0 - sig)))
        pg_out[:, at] = d_gate.astype(bf16)
        bg[:, at] = d_full
        low_dy[:, at] = d_full.astype(bf16)
        skip_sum.append(jnp.sum(d_full * act[:, at], axis=0, keepdims=True))
    turned_dy[...] = turned(low_dy[...])
    turned_branch[...] = turned(branch_out[...])
    send_mixed()

    d_scores[...] = jnp.zeros((SEQ, SEQ), f32)

    @pl.loop(0, 8)
    def _(p):
        for e in range(2):
            head = 2 * p + e
            own = pl.ds(pl.multiple_of(64 * head, 64), 64)
            sums = [None, None]
            for i in range(2):
                at_i = slice(256 * i, 256 * i + 256)
                out_grad = low_dy[at_i, tile(p)]
                keep = left_lanes if e == 0 else ~left_lanes
                out_grad = jnp.where(keep, out_grad, jnp.zeros_like(out_grad))
                for j in range(i + 1):
                    near = decay(head, i, j)
                    weight = (near * scores[block(i, j)]).astype(bf16)
                    d_weight = dot(out_grad, low_x[256 * j : 256 * j + 256, tile(p)], (1, 1))
                    d_scores[block(i, j)] += d_weight * near
                    term = dot(turned_dy[own, at_i], weight)
                    sums[j] = term if sums[j] is None else sums[j] + term
            for j in range(2):
                turned_dx[own, 256 * j : 256 * j + 256] = sums[j]

    d_x = turned(turned_dx[...])
    dots = low_dy[...].astype(f32) * y[...] - low_x[...].astype(f32) * d_x
    d_run = pick(dots, expand, 3, 1)
    up = jnp.where(rows <= cols, 1.0, 0.0).astype(bf16)
    d_log = summed(up, d_run)
    d_step = pick(d_x * act[:, 0:OWN], expand, 2, 1) + d_log * rate
    d_raw = d_step * jax.nn.sigmoid(raw)
    pg_out[:, 2304:2432] = d_raw.astype(bf16)
    skip_row = pick(jnp.broadcast_to(jnp.concatenate(skip_sum, axis=1), (8, OWN)), expand, 3, 1)[0:1]
    for half in range(2):
        base = 512 * half
        strip[base + 57 : base + 58, :] = jnp.sum(d_raw, axis=0, keepdims=True)
        strip[base + 58 : base + 59, :] = jnp.sum(d_log * step, axis=0, keepdims=True) * rate
        strip[base + 59 : base + 60, :] = skip_row
    d_b = near_exact(turned(d_scores[...]), c_mat, 0)
    d_c = near_exact(d_scores[...], b_mat, 0)
    act[:, 0:OWN] = d_x * step_wide + bg[...] * skip_wide
    act[:, 1024:1152] = d_b
    act[:, 1152:1280] = d_c

    @pl.loop(0, 10)
    def _(j):
        value = proj[:, pl.ds(pl.multiple_of(1024 + 128 * j, 128), 128)]
        before = pre[:, tile(j)]
        sig = jax.nn.sigmoid(before)
        d_pre = act[:, tile(j)] * (sig * (1.0 + before * (1.0 - sig)))
        total = vec[3:4, tile(j)] * d_pre
        full_tile = jnp.where(j < 8, 8 * grp + j, 8 + j)
        half = full_tile // 9
        base = 512 * half + full_tile - 9 * half
        strip[pl.ds(base + 31, 1), :] = jnp.sum(d_pre * value, axis=0, keepdims=True)
        strip[pl.ds(base + 40, 1), :] = jnp.sum(d_pre, axis=0, keepdims=True)
        for k in range(1, 4):
            kept = pltpu.roll(d_pre * same[k - 1], SEQ - k, 0)
            total = total + vec[3 - k : 4 - k, tile(j)] * kept
            strip[pl.ds(base + 4 + 9 * (3 - k), 1), :] = jnp.sum(
                kept * value, axis=0, keepdims=True
            )
        pg_out[:, pl.ds(pl.multiple_of(1024 + 128 * j, 128), 128)] = total.astype(bf16)

    pg_out[:, HELD:] = jnp.zeros((SEQ, 128), bf16)
    turned_pg[...] = turned(pg_out[...])
    send_pg()
    normed_grad = dot(pg_out[...], w_in[...])
    ng_out[...] = normed_grad.astype(ng_out.dtype)
    inputs = tokens[...].astype(f32)
    scale = lax.rsqrt(jnp.mean(inputs * inputs, axis=1, keepdims=True) + EPS)
    gain_row = jnp.sum(normed_grad * (inputs * scale), axis=0, keepdims=True)
    for j in range(8):
        strip[512 * (j // 4) + j % 4 : 512 * (j // 4) + j % 4 + 1, :] = gain_row[
            :, 128 * j : 128 * j + 128
        ]
    strip_out[...] = turned(strip[...]).astype(bf16)
    vecs_out[0] = strip[0:64, :]
    vecs_out[1] = strip[512:576, :]


def layer_body(
    tokens, seg, small, w_in, w_out, cot_own,
    turned_branch, mixed_out, turned_pg, ng_out, strip_out, normed_out, cot_out, vecs_out,
    far_branch, far_pg, far_normed, far_cot,
    branch_out, pg_out, proj, vec, words, sent_mixed, far_mixed, *scratch,
):
    f32, bf16 = jnp.float32, jnp.bfloat16
    send_sems, recv_sems = scratch[-2:]
    scratch = scratch[:-2]
    stats, far_stats = scratch[-2:]
    here = place()
    grp = here["grp"]
    across = device_at(moved(here, "z", 2))
    twin = twin_of(here)
    theirs = 1 - here["core"]
    greet([across, twin])
    copies = Copies(send_sems, recv_sems)
    own_rows = pl.ds(pl.multiple_of(256 * grp, 256), 256)
    far_rows = pl.ds(pl.multiple_of(256 * (1 - grp), 256), 256)
    cot_in = copies.start(cot_own, cot_out.at[own_rows, :], across)
    cot_out[own_rows, :] = cot_own[...]

    words[...] = small[...].astype(f32)
    for j in range(10):
        if j < 8:
            half = lax.div(8 * grp + j, 9)
            at = 8 * grp + j - 9 * half
        else:
            half, at = 1, j - 1
        for k in range(5):
            vec[k : k + 1, 128 * j : 128 * j + 128] = words[half, pl.ds(4 + 9 * k + at, 1), :]
        if j < 8:
            vec[5:6, 128 * j : 128 * j + 128] = words[grp, 49 + j : 50 + j, :]
            vec[9:10, 128 * j : 128 * j + 128] = words[j // 4, j % 4 : j % 4 + 1, :]
    for k in range(3):
        vec[6 + k : 7 + k, 0:128] = words[0, 57 + k : 58 + k, :] + words[1, 57 + k : 58 + k, :]
    inputs = tokens[...].astype(f32)
    scale = lax.rsqrt(jnp.mean(inputs * inputs, axis=1, keepdims=True) + EPS)
    normed_out[...] = (inputs * scale * vec[9:10, 0:1024]).astype(bf16)

    held = {"normed": copies.start(normed_out, far_normed, twin)}

    @pl.loop(0, 9)
    def _(j):
        at = pl.ds(pl.multiple_of(256 * j, 256), 256)
        proj[:, at] = dot(normed_out[...], w_in[at, :], (1, 1))

    proj[:, 2304:2432] = dot(normed_out[...], w_in[2304:2432, :], (1, 1))

    def cot_ready():
        cot_in.wait_recv()
        half = pl.ds(pl.multiple_of(512 * theirs, 512), 512)
        held["cot"] = copies.start(cot_out.at[:, half], far_cot, twin)

    def exchange():
        copy = copies.start(stats, far_stats, across)
        copy.wait_recv()

    def send_pg():
        rows = pl.ds(pl.multiple_of(1280 * theirs, 1280), 1280)
        held["pg"] = copies.start(turned_pg.at[rows, :], far_pg, twin)

    def send_mixed():
        held["branch"] = copies.start(turned_branch, far_branch, twin)
        sent_mixed[...] = dot(branch_out[far_rows, :], w_out[...]).astype(bf16)
        held["mixed"] = copies.start(sent_mixed, far_mixed, across)

    layer_kernel(
        grp, cot_ready, exchange, send_mixed, send_pg, proj, vec, seg, tokens, cot_out, w_out, w_in,
        branch_out, pg_out, ng_out, strip_out, vecs_out, turned_branch, turned_pg, *scratch,
    )
    held["mixed"].wait_recv()
    total = dot(branch_out[own_rows, :], w_out[...]) + far_mixed[...].astype(f32)
    total = total + tokens[own_rows, :].astype(f32)
    mixed_out[...] = total.astype(bf16)
    for name in ("normed", "cot", "branch", "pg"):
        held[name].wait_recv()
    copies.finish()


def layer_grads(tokens, seg, small, w_in, w_out, cotangent):
    f32, bf16 = jnp.float32, jnp.bfloat16
    shape = jax.ShapeDtypeStruct
    spec = pl.BlockSpec(memory_space=pltpu.VMEM)
    scratch = [
        pltpu.VMEM((SEQ, OWN), bf16),
        pltpu.VMEM((SEQ, 2560), bf16),
        pltpu.VMEM((SEQ, HELD), f32),
        pltpu.VMEM((16, MIX), f32),
        pltpu.VMEM((2, 64, 128), f32),
        pltpu.VMEM((256, 1024), bf16),
        pltpu.VMEM((256, 1024), bf16),
    ]
    return pl.pallas_call(
        layer_body,
        out_shape=[
            shape((OWN, SEQ), bf16),
            shape((256, 1024), bf16),
            shape((2560, SEQ), bf16),
            shape((SEQ, 1024), bf16),
            shape((128, 1024), bf16),
            shape((SEQ, 1024), bf16),
            shape((SEQ, 1024), bf16),
            shape((2, 64, 128), f32),
            shape((OWN, SEQ), bf16),
            shape((1280, SEQ), bf16),
            shape((SEQ, 1024), bf16),
            shape((SEQ, 512), bf16),
        ],
        in_specs=[spec] * 6,
        out_specs=[spec] * 8 + [pl.BlockSpec(memory_space=pl.ANY)] * 4,
        scratch_shapes=scratch + layer_scratch() + copy_sems(8),
        compiler_params=pltpu.CompilerParams(
            collective_id=1, has_side_effects=True, vmem_limit_bytes=62 * 1024 * 1024
        ),
        name="layer_grads",
    )(tokens, seg, small, w_in, w_out, cotangent)


def layer_scratch():
    f32, bf16 = jnp.float32, jnp.bfloat16
    return [
        pltpu.VMEM((SEQ, MIX), f32),
        pltpu.VMEM((SEQ, MIX), f32),
        pltpu.VMEM((3, SEQ, 128), f32),
        pltpu.VMEM((SEQ, 2048), f32),
        pltpu.VMEM((128, SEQ), f32),
        pltpu.VMEM((SEQ, SEQ), f32),
        pltpu.VMEM((SEQ, SEQ), f32),
        pltpu.VMEM((SEQ, OWN), bf16),
        pltpu.VMEM((SEQ, OWN), f32),
        pltpu.VMEM((SEQ, OWN), f32),
        pltpu.VMEM((SEQ, OWN), bf16),
        pltpu.VMEM((OWN, SEQ), bf16),
        pltpu.VMEM((OWN, SEQ), f32),
        pltpu.VMEM((SEQ, SEQ), f32),
        pltpu.VMEM((1024, 128), f32),
        pltpu.VMEM((8, SEQ), f32),
        pltpu.VMEM((8, SEQ), f32),
    ]


MESH = pl.DeviceIdType.MESH


def place():
    rep, grp = lax.axis_index("rep"), lax.axis_index("grp")
    return {
        "core": lax.rem(rep, 2),
        "x": lax.rem(lax.div(rep, 2), 4),
        "y": lax.rem(lax.div(rep, 8), 4),
        "z": 2 * grp + lax.div(rep, 32),
        "low": lax.div(rep, 32),
        "grp": grp,
    }


def device_at(here):
    low_z = lax.rem(here["z"], 2)
    rep = ((low_z * 4 + here["y"]) * 4 + here["x"]) * 2 + here["core"]
    return (rep, lax.div(here["z"], 2))


def moved(here, axis, by):
    return dict(here, **{axis: lax.rem(here[axis] + (by % 4), 4)})


def twin_of(here):
    return device_at(dict(here, core=1 - here["core"]))


def mate_of(here):
    return device_at(dict(here, z=here["z"] + 1 - 2 * here["low"]))


def greet(partners):
    barrier = pltpu.get_barrier_semaphore()
    for partner in partners:
        pl.semaphore_signal(barrier, inc=1, device_id=partner, device_id_type=MESH)
    pl.semaphore_wait(barrier, len(partners))


class Copies:
    def __init__(self, send_sems, recv_sems):
        self.send_sems, self.recv_sems = send_sems, recv_sems
        self.made = []

    def start(self, src, dst, device):
        at = len(self.made)
        copy = pltpu.make_async_remote_copy(
            src_ref=src,
            dst_ref=dst,
            send_sem=self.send_sems.at[at],
            recv_sem=self.recv_sems.at[at],
            device_id=device,
            device_id_type=MESH,
        )
        copy.start()
        self.made.append(copy)
        return copy

    def finish(self):
        for copy in self.made:
            copy.wait_send()


def copy_sems(count):
    return [pltpu.SemaphoreType.DMA((count,)), pltpu.SemaphoreType.DMA((count,))]


def cut_in_two(axes, free, sizes):
    if not free:
        return (axes, None)
    name = free[0]
    half = sizes[name] // 2
    return (
        dict(axes, **{name: slice(0, half)}),
        dict(axes, **{name: slice(half, 2 * half)}),
    )


class Spread:
    def __init__(self, copies, here, order, view, sizes, others):
        self.copies, self.here, self.order, self.view, self.sizes = copies, here, order, view, sizes
        self.own = {"x": here["x"], "y": here["y"], "z": here["low"]}
        self.own = {name: self.own[name] for name in order + others}
        self.twin = twin_of(here)
        self.to_twin = []

    def axes(self, stage, at):
        axes = dict(self.own)
        for name in self.order[:stage]:
            axes[name] = slice(None)
        axes[self.order[stage]] = at
        return axes

    def free(self, stage):
        return [name for name in ("x", "y", "z") if name in self.order[:stage]]

    def share(self, stage, at):
        if stage == len(self.order) - 1:
            piece = self.view(self.axes(stage, at))
            self.to_twin.append(self.copies.start(piece, piece, self.twin))

    def begin(self, stage):
        axis = self.order[stage]
        at = self.own[axis]
        piece = self.view(self.axes(stage, at))
        if axis == "z":
            self.first = (self.copies.start(piece, piece, mate_of(self.here)),)
        else:
            self.first = (
                self.copies.start(piece, piece, device_at(moved(self.here, axis, 1))),
                self.copies.start(piece, piece, device_at(moved(self.here, axis, -1))),
            )
        self.share(stage, at)

    def forward(self, stage):
        axis = self.order[stage]
        self.second = []
        if axis == "z":
            self.first[0].wait_recv()
            self.share(stage, 1 - self.own[axis])
            return
        free = self.free(stage)
        before, after = lax.rem(self.own[axis] + 3, 4), lax.rem(self.own[axis] + 1, 4)
        self.first[0].wait_recv()
        low, _ = cut_in_two(self.axes(stage, before), free, self.sizes)
        piece = self.view(low)
        self.second.append(self.copies.start(piece, piece, device_at(moved(self.here, axis, 1))))
        self.share(stage, before)
        self.first[1].wait_recv()
        if free:
            _, high = cut_in_two(self.axes(stage, after), free, self.sizes)
            piece = self.view(high)
            self.second.append(
                self.copies.start(piece, piece, device_at(moved(self.here, axis, -1)))
            )
        self.share(stage, after)

    def complete(self, stage):
        for copy in self.second:
            copy.wait_recv()
        if self.order[stage] != "z":
            self.share(stage, lax.rem(self.own[self.order[stage]] + 2, 4))


def gather_kernel(
    w_ref, small_ref, seg_ref, tok_ref, w_out, small_out, seg_out, tok_out,
    staged, relayed, local_sems, send_sems, recv_sems,
):
    here = place()
    grp, core = here["grp"], here["core"]
    away = 1 - grp
    across = device_at(moved(here, "z", 2))
    beside = device_at(dict(here, z=3 - here["z"]))
    ring = [device_at(moved(here, axis, by)) for axis in ("x", "y") for by in (1, -1)]
    lanes = lambda half, first, width: pl.ds(pl.multiple_of(512 * half + first, 128), width)

    kept = []

    def keep(owner, dst):
        for start, rows, at in ((1024 * owner, 1024, 0), (2048 + 1024 * owner, 1024, 1024), (4096, 288, 2048)):
            src = w_ref.at[pl.ds(pl.multiple_of(start, 32), rows), :]
            copy = pltpu.make_async_copy(src, dst(pl.ds(at, rows)), local_sems.at[len(kept)])
            copy.start()
            kept.append(copy)

    keep(away, lambda rows: staged.at[rows, :])
    keep(grp, lambda rows: w_out.at[rows, lanes(grp, 0, 512)])
    staged[2336:2560, :] = jnp.zeros((224, 512), jnp.bfloat16)
    w_out[2336:2560, lanes(grp, 0, 512)] = jnp.zeros((224, 512), jnp.bfloat16)
    by_core = 1 + 2 * core
    onward = device_at(dict(here, z=lax.rem(here["z"] + by_core, 4)))
    sides = [device_at(moved(here, "z", by)) for by in (1, -1)]
    greet([across, twin_of(here)] + sides + ring)
    copies = Copies(send_sems, recv_sems)
    tok_rows = pl.ds(pl.multiple_of(256 * grp, 256), 256)
    for copy in kept[0:3]:
        copy.wait()
    orders = (("y", "x"), ("x", "y"))

    def rows_of(part, axes):
        minor, major = orders[part]
        start, count = axes[minor], 1
        if isinstance(start, slice):
            bounds = start.indices(4)
            start, count = bounds[0], bounds[1] - bounds[0]
        return pl.ds(
            pl.multiple_of(1280 * core + 320 * axes[major] + 80 * start, 16), 80 * count
        )

    pieces = []
    for part in range(2):
        rows = rows_of(part, here)
        pieces.append(
            copies.start(
                staged.at[rows, pl.ds(256 * part, 256)],
                w_out.at[rows, lanes(grp, 256 * part, 256)],
                beside,
            )
        )
    quarter = lambda at: pl.ds(64 * at, 64)
    tok_hops = [
        copies.start(tok_ref.at[quarter(at), :], relayed.at[quarter(at), :], onward)
        for at in range(4)
    ]
    tok_in = []

    def relay(at):
        tok_hops[at].wait_recv()
        owner = lax.div(lax.rem(here["z"] + 4 - by_core, 4), 2)
        rows = pl.ds(pl.multiple_of(256 * owner + 64 * at, 64), 64)
        tok_in.append(copies.start(relayed.at[quarter(at), :], tok_out.at[rows, :], onward))

    small_in = copies.start(small_ref, small_out.at[grp], beside)
    seg_in = copies.start(seg_ref, seg_out.at[:, tok_rows], across)
    tok_out[tok_rows, :] = tok_ref[...]
    small_out[grp] = small_ref[...]
    seg_out[:, tok_rows] = seg_ref[...]
    sizes = {"x": 4, "y": 4}
    parts = []
    for part in range(2):

        def view(axes, part=part):
            return w_out.at[rows_of(part, axes), lanes(away, 256 * part, 256)]

        parts.append(Spread(copies, here, orders[part], view, sizes, ()))
    for piece in pieces:
        piece.wait_recv()
    for stage in range(2):
        for part in parts:
            part.begin(stage)
        relay(2 * stage)
        for part in parts:
            part.forward(stage)
        relay(2 * stage + 1)
        for part in parts:
            part.complete(stage)
    for part in parts:
        for copy in part.to_twin:
            copy.wait_recv()
    for copy in tok_in + [small_in, seg_in]:
        copy.wait_recv()
    for copy in kept[3:]:
        copy.wait()
    copies.finish()


def gather(w_in, small, seg, tokens):
    bf16 = jnp.bfloat16
    vmem = pl.BlockSpec(memory_space=pltpu.VMEM)
    return pl.pallas_call(
        gather_kernel,
        out_shape=[
            jax.ShapeDtypeStruct((2560, 1024), bf16),
            jax.ShapeDtypeStruct((2, 64, 128), bf16),
            jax.ShapeDtypeStruct((8, SEQ), jnp.int32),
            jax.ShapeDtypeStruct((SEQ, 1024), bf16),
        ],
        in_specs=[pl.BlockSpec(memory_space=pl.ANY)] + [vmem] * 3,
        out_specs=[vmem] * 4,
        scratch_shapes=[pltpu.VMEM((2560, 512), bf16), pltpu.VMEM((256, 1024), bf16), pltpu.SemaphoreType.DMA((6,))] + copy_sems(40),
        compiler_params=pltpu.CompilerParams(
            collective_id=0, has_side_effects=True, vmem_limit_bytes=60 * 1024 * 1024
        ),
        name="gather",
    )(w_in.T, small, seg, tokens)


W_PARTS = (("x", "y"), ("y", "x"))


def reduce_kernel(
    normed_ref, pg_ref, branch_ref, cot_ref, strip_ref, ng_ref,
    far_branch_ref, far_pg_ref, far_normed_ref, far_cot_ref, out_w, out_o, far_ng,
    near_normed, near_pg, near_branch, near_cot, near_strip,
    far_normed, far_pg, far_branch, far_cot, far_strip, buf_w, buf_o,
    half_0, whole_0, half_1, whole_1, last, half_o, whole_o, pair_o, last_o,
    local_sems, send_sems, recv_sems,
):
    f32, bf16 = jnp.float32, jnp.bfloat16
    here = place()
    grp, core, low = here["grp"], here["core"], here["low"]
    twin, mate = twin_of(here), mate_of(here)
    crossing = [device_at(moved(here, "z", by)) for by in (1, 2, 3)]
    ring = [device_at(moved(here, axis, by)) for axis in ("x", "y") for by in (1, -1)]
    greet([twin] + crossing + ring)
    copies = Copies(send_sems, recv_sems)

    loads = []
    for at, (src, dst) in enumerate(
        (
            (branch_ref, near_branch),
            (cot_ref.at[:, pl.ds(pl.multiple_of(512 * core, 512), 512)], near_cot),
            (far_branch_ref, far_branch),
            (far_cot_ref, far_cot),
            (normed_ref, near_normed),
            (far_normed_ref, far_normed),
            (far_pg_ref, far_pg),
            (pg_ref.at[pl.ds(pl.multiple_of(1280 * core, 1280), 1280), :], near_pg),
            (strip_ref, near_strip),
        )
    ):
        loads.append(pltpu.make_async_copy(src, dst, local_sems.at[at]))
        loads[-1].start()
    my_half = pl.ds(pl.multiple_of(512 * core, 512), 512)
    strip_in = copies.start(strip_ref, far_strip, twin)

    sizes = {"x": 4, "y": 4, "z": 4}

    def ring_axes(axis, axes, by):
        return dict(axes, **{axis: lax.rem(here[axis] + (by % 4), 4)})

    class RingSum:
        def __init__(self, axis, axes, free, view, load, store, halved, whole):
            self.axis, self.axes, self.free = axis, axes, free
            self.view, self.load, self.store = view, load, store
            self.halved, self.whole = halved, whole
            self.ahead = device_at(moved(here, axis, 1))
            self.behind = device_at(moved(here, axis, -1))

        def chunk(self, by):
            return ring_axes(self.axis, self.axes, by)

        def begin(self):
            first, second = cut_in_two(self.chunk(2), self.free, sizes)
            if self.free:
                self.a = copies.start(self.view(first), self.halved.at[0], self.ahead)
                self.b = copies.start(self.view(second), self.halved.at[1], self.behind)
                _, second = cut_in_two(self.chunk(1), self.free, sizes)
                first, _ = cut_in_two(self.chunk(-1), self.free, sizes)
                self.waits = [
                    copies.start(self.view(second), self.whole.at[0, pl.ds(2, 2)], self.ahead),
                    copies.start(self.view(first), self.whole.at[1, pl.ds(0, 2)], self.behind),
                ]
            else:
                self.a = copies.start(self.view(first), self.whole.at[2], self.ahead)
                self.waits = [copies.start(self.view(self.chunk(-1)), self.whole.at[1], self.behind)]

        def add(self, axes, incoming):
            total = self.load(axes).astype(f32)
            for value in incoming:
                total = total + value.astype(f32)
            self.store(axes, total.astype(bf16))

        def relay(self):
            self.a.wait_recv()
            if self.free:
                first, _ = cut_in_two(self.chunk(1), self.free, sizes)
                self.add(first, [self.halved[0]])
                self.waits.append(
                    copies.start(self.view(first), self.whole.at[0, pl.ds(0, 2)], self.ahead)
                )
                self.b.wait_recv()
                _, second = cut_in_two(self.chunk(-1), self.free, sizes)
                self.add(second, [self.halved[1]])
                self.waits.append(
                    copies.start(self.view(second), self.whole.at[1, pl.ds(2, 2)], self.behind)
                )
            else:
                self.add(self.chunk(1), [self.whole[2]])
                self.waits.append(
                    copies.start(self.view(self.chunk(1)), self.whole.at[0], self.ahead)
                )

        def settle(self):
            for copy in self.waits:
                copy.wait_recv()
            self.add(self.chunk(0), [self.whole[0], self.whole[1]])

    def w_ring(part, stage):
        order = W_PARTS[part]
        axes = {"z": slice(None)}
        if stage == 0:
            axes[order[1]] = slice(None)
        else:
            axes[order[0]] = here[order[0]]
        free = [name for name in ("x", "y", "z") if name in axes and isinstance(axes[name], slice)]
        index = lambda axes: (part, axes["x"], axes["y"], axes["z"])

        def load(axes):
            return buf_w[index(axes)]

        def store(axes, value):
            buf_w[index(axes)] = value

        half, whole = ((half_0, whole_0), (half_1, whole_1))[stage]
        return RingSum(
            order[stage], axes, free, lambda axes: buf_w.at[index(axes)], load, store,
            half.at[part], whole.at[part],
        )

    def o_ring(stage):
        axis = ("x", "y")[stage]
        axes = {"y": slice(None)} if stage == 0 else {"x": here["x"]}
        free = ["y"] if stage == 0 else []
        index = lambda axes: (axes["x"], axes["y"], low)

        def load(axes):
            return buf_o[index(axes)]

        def store(axes, value):
            buf_o[index(axes)] = value

        return RingSum(
            axis, axes, free, lambda axes: buf_o.at[index(axes)], load, store,
            half_o, (whole_o, last_o)[stage],
        )

    for copy in loads[0:4]:
        copy.wait()

    @pl.loop(0, 4)
    def _(row):
        at = pl.ds(pl.multiple_of(256 * row, 256), 256)
        value = dot(near_branch[at, :], near_cot[...])
        value = value + dot(far_branch[at, :], far_cot[...])
        buf_o[row] = value.astype(bf16).reshape(4, 2, 32, 512)

    pair_in = copies.start(buf_o.at[:, :, 1 - low], pair_o, mate)

    for copy in loads[4:]:
        copy.wait()
    strip_in.wait_recv()

    def w_rows(row):
        rows = pl.ds(pl.multiple_of(320 * row, 16), 320)
        return dot(near_pg[rows, :], near_normed[...]) + dot(far_pg[rows, :], far_normed[...])

    def w_store(row, value):
        for part in range(2):
            for z in range(4):
                tile = value[:, 256 * z + 128 * part : 256 * z + 128 * part + 128]
                buf_w[part, row, :, z] = tile.astype(bf16).reshape(4, 80, 128)

    @pl.loop(0, 3)
    def _(row):
        w_store(row, w_rows(row))

    value = w_rows(3)
    small = near_strip[...].astype(f32) + far_strip[...].astype(f32)
    tail = value[192:, :] + small * core.astype(f32)
    w_store(3, jnp.concatenate([value[:192, :], tail], axis=0))
    rings = []
    for part in range(2):
        rings.append(w_ring(part, 0))
        rings[-1].begin()

    pair_in.wait_recv()

    @pl.loop(0, 4)
    def _(row):
        total = buf_o[row, :, low].astype(f32) + pair_o[row].astype(f32)
        buf_o[row, :, low] = total.astype(bf16)

    their_tokens = pl.ds(pl.multiple_of(256 * (1 - grp), 256), 256)
    ng_in = copies.start(ng_ref.at[their_tokens, :], far_ng, crossing[1])
    o_part = o_ring(0)
    o_part.begin()
    for ring_sum in rings:
        ring_sum.relay()
    o_part.relay()
    later = []
    for part in range(2):
        rings[part].settle()
        later.append(w_ring(part, 1))
        later[-1].begin()
    o_part.settle()
    o_part = o_ring(1)
    o_part.begin()
    for ring_sum in later:
        ring_sum.relay()
    o_part.relay()

    across = []
    for part in range(2):
        later[part].settle()
        across.append(
            [
                copies.start(
                    buf_w.at[part, here["x"], here["y"], lax.rem(here["z"] + by, 4)],
                    last.at[part, by - 1],
                    crossing[by - 1],
                )
                for by in (1, 2, 3)
            ]
        )
    o_part.settle()
    out_o[here["x"], here["y"], low, :, my_half] = buf_o[here["x"], here["y"], low]
    o_view = lambda axes: out_o.at[axes["x"], axes["y"], axes["z"], :, my_half]
    out_sizes = {"x": 4, "y": 4, "z": 2}
    o_spread = Spread(copies, here, ("y", "x", "z"), o_view, out_sizes, ())
    o_spread.begin(0)
    spreads = []
    for part in range(2):
        for copy in across[part]:
            copy.wait_recv()
        mine = buf_w[part, here["x"], here["y"], here["z"]].astype(f32)
        mine = mine + last[part, 2 - 2 * low].astype(f32)
        other = last[part, 1].astype(f32) + last[part, 2 * low].astype(f32)
        out_w[grp, core, here["x"], here["y"], low, part] = mine.astype(bf16)
        out_w[1 - grp, core, here["x"], here["y"], low, part] = other.astype(bf16)

        def w_view(axes, part=part):
            return out_w.at[:, core, axes["x"], axes["y"], axes["z"], part]

        order = ("z",) + W_PARTS[part][::-1]
        spreads.append(Spread(copies, here, order, w_view, out_sizes, ()))
        spreads[-1].begin(0)
    spreads.append(o_spread)
    for stage in range(3):
        if stage > 0:
            for spread in spreads:
                spread.begin(stage)
        for spread in spreads:
            spread.forward(stage)
        for spread in spreads:
            spread.complete(stage)
    for spread in spreads:
        for copy in spread.to_twin:
            copy.wait_recv()
    ng_in.wait_recv()
    copies.finish()


def reduce_gradients(normed, proj_grad, branch, cotangent, strip, ng, far):
    bf16 = jnp.bfloat16
    vmem = lambda *shape: pltpu.VMEM(shape, bf16)
    spec = pl.BlockSpec(memory_space=pltpu.VMEM)
    scratch = 2 * [
        vmem(SEQ, 1024),
        vmem(1280, SEQ),
        vmem(OWN, SEQ),
        vmem(SEQ, 512),
        vmem(128, 1024),
    ]
    scratch += [
        vmem(2, 4, 4, 4, 80, 128),
        vmem(4, 4, 2, 32, 512),
        vmem(2, 2, 2, 4, 80, 128),
        vmem(2, 2, 4, 4, 80, 128),
        vmem(2, 2, 2, 80, 128),
        vmem(2, 2, 4, 80, 128),
        vmem(2, 3, 80, 128),
        vmem(2, 2, 32, 512),
        vmem(2, 4, 32, 512),
        vmem(4, 4, 32, 512),
        vmem(3, 32, 512),
    ]
    return pl.pallas_call(
        reduce_kernel,
        out_shape=[
            jax.ShapeDtypeStruct((2, 2, 4, 4, 2, 2, 80, 128), bf16),
            jax.ShapeDtypeStruct((4, 4, 2, 32, 1024), bf16),
            jax.ShapeDtypeStruct((256, 1024), bf16),
        ],
        in_specs=[pl.BlockSpec(memory_space=pl.ANY)] * 10,
        out_specs=[spec] * 3,
        scratch_shapes=scratch + [pltpu.SemaphoreType.DMA((9,))] + copy_sems(110),
        compiler_params=pltpu.CompilerParams(
            collective_id=2, has_side_effects=True, vmem_limit_bytes=60 * 1024 * 1024
        ),
        name="reduce_gradients",
    )(normed, proj_grad, branch, cotangent, strip, ng, *far)

def finish_kernel(
    sum_w, sum_o, ng, far_ng, tokens, cot, small, mixed, vecs_ref,
    w_in_out, w_out_out, input_out, mixed_out, gain_out, conv_w_out, conv_b_out, heads_out, gate_out,
    loaded_w, loaded_o, gate_rows, x_rows, end_rows, o_rows, sems,
):
    f32 = jnp.float32
    grp = lax.axis_index("grp")
    loads = [
        pltpu.make_async_copy(sum_o, loaded_o, sems.at[4]),
        pltpu.make_async_copy(sum_w, loaded_w, sems.at[5]),
    ]
    for copy in loads:
        copy.start()
    started = []

    def send(src, dst):
        copy = pltpu.make_async_copy(src, dst, sems.at[len(started)])
        copy.start()
        started.append(copy)

    def block(own, at):
        core, x, y = at // 16, at // 4 % 4, at % 4
        return lambda q: loaded_w[own, core, x, y, q // 2, q % 2]

    def fill(ref, own, base, first, last):
        for at in range(first // 80, -(-last // 80)):
            low, high = max(first, 80 * at), min(last, 80 * at + 80)
            for q in range(4):
                part = block(own, at)(q)[low - 80 * at : high - 80 * at].astype(f32)
                ref[base + low - first : base + high - first, 128 * q : 128 * q + 128] = part

    own_rows = pl.ds(pl.multiple_of(256 * grp, 256), 256)
    words = small[...].astype(f32)
    gain = jnp.concatenate([words[j // 4, j % 4 : j % 4 + 1] for j in range(8)], axis=1)
    inputs = tokens[...].astype(f32)
    scale = lax.rsqrt(jnp.mean(inputs * inputs, axis=1, keepdims=True) + EPS)
    scaled = (ng[own_rows, :].astype(f32) + far_ng[...].astype(f32)) * gain
    inner = jnp.mean(scaled * inputs, axis=1, keepdims=True)
    input_out[...] = cot[...].astype(f32) + scale * (scaled - inputs * (scale * scale * inner))
    mixed_out[...] = mixed[...]
    loads[0].wait()
    for row in range(4):
        o_rows[256 * row : 256 * row + 256, :] = loaded_o[row].reshape(256, 1024).astype(f32)
    send(o_rows, w_out_out)
    loads[1].wait()
    for own in range(2):
        fill(gate_rows, own, 1024 * own, 0, 1024)
    send(gate_rows, w_in_out.at[pl.ds(0, 2048), :])
    for own in range(2):
        fill(x_rows, own, 1024 * own, 1024, 2048)
    send(x_rows, w_in_out.at[pl.ds(2048, 2048), :])
    fill(end_rows, 0, 0, 2048, 2560)
    for at in range(25, 32):
        low = max(2048, 80 * at)
        for q in range(4):
            part = block(1, at)(q)[low - 80 * at :].astype(f32)
            end_rows[low - 2048 : 80 * at + 80 - 2048, 128 * q : 128 * q + 128] += part
    send(end_rows.at[pl.ds(0, 288), :], w_in_out.at[pl.ds(4096, 288), :])
    vecs = vecs_ref[...]
    for j in range(4):
        gain_out[j : j + 1, :] = vecs[j : j + 1]
        for k in range(9):
            conv_w_out[j : j + 1, 128 * k : 128 * k + 128] = vecs[4 + 9 * j + k : 5 + 9 * j + k]
    for k in range(9):
        conv_b_out[0:1, 128 * k : 128 * k + 128] = vecs[40 + k : 41 + k]
    gate_out[...] = vecs[49:57]
    heads = vecs[56:64]
    heads_out[...] = jnp.where(grp == 0, heads, pltpu.roll(heads, 112, 1))

    for copy in started:
        copy.wait()


def finish(sum_w, sum_o, ng, far_ng, tokens, cot, small, mixed, vecs):
    f32 = jnp.float32
    shape = jax.ShapeDtypeStruct
    spec = pl.BlockSpec(memory_space=pltpu.VMEM)
    away = pl.BlockSpec(memory_space=pl.ANY)
    return pl.pallas_call(
        finish_kernel,
        out_shape=[
            shape((4384, 512), f32),
            shape((1024, 1024), f32),
            shape((256, 1024), f32),
            shape((256, 1024), jnp.bfloat16),
            shape((4, 128), f32),
            shape((4, 1152), f32),
            shape((1, 1152), f32),
            shape((8, 128), f32),
            shape((8, 128), f32),
        ],
        in_specs=[away] * 2 + [spec] * 7,
        out_specs=[away] * 2 + [spec] * 7,
        scratch_shapes=[
            pltpu.VMEM((2, 2, 4, 4, 2, 2, 80, 128), jnp.bfloat16),
            pltpu.VMEM((4, 4, 2, 32, 1024), jnp.bfloat16),
            pltpu.VMEM((2048, 512), f32),
            pltpu.VMEM((2048, 512), f32),
            pltpu.VMEM((512, 512), f32),
            pltpu.VMEM((1024, 1024), f32),
            pltpu.SemaphoreType.DMA((6,)),
        ],
        compiler_params=pltpu.CompilerParams(vmem_limit_bytes=60 * 1024 * 1024),
        name="finish",
    )(sum_w, sum_o, ng, far_ng, tokens, cot, small, mixed, vecs)


def on_device(
    tokens, segments, in_gain, w_in, conv_w, conv_b, dt_bias, a_log, d_skip, gate_gain, w_out,
    cotangent,
):
    bf16 = jnp.bfloat16
    grp = lax.axis_index("grp")
    heads = jnp.stack([dt_bias, a_log, d_skip]).astype(jnp.float32)
    heads = jnp.where(grp == 0, jnp.pad(heads, ((0, 0), (0, 112))), jnp.pad(heads, ((0, 0), (16, 96))))
    rows = [
        in_gain.reshape(4, 128),
        conv_w.reshape(36, 128),
        conv_b.reshape(9, 128),
        gate_gain.reshape(8, 128),
        heads,
    ]
    small, at = 0.0, 0
    for part in rows:
        count = part.shape[0]
        small = small + jnp.pad(part.astype(jnp.float32), ((at, 64 - at - count), (0, 0)))
        at += count
    small = small.astype(bf16)
    seg = jnp.broadcast_to(segments[None], (8, 256))
    w_held, small_all, seg_all, tok_all = gather(w_in, small, seg, tokens)
    branch, mixed, pg, ng, strip, normed, cot_all, vecs, *far = layer_grads(
        tok_all, seg_all, small_all, w_held, w_out, cotangent
    )
    vecs = lax.dynamic_index_in_dim(lax.psum(vecs, ("rep", "grp")), grp, 0, False)
    sum_w, sum_o, far_ng = reduce_gradients(normed, pg, branch, cot_all, strip, ng, far)
    w_in_t, w_out_grad, input_grad, mixed, gain, conv_w_grad, conv_b_grad, per_head, gate = finish(
        sum_w, sum_o, ng, far_ng, tokens, cotangent, small_all, mixed, vecs
    )
    return (
        mixed,
        input_grad,
        gain.reshape(512),
        w_in_t.T,
        conv_w_grad,
        conv_b_grad.reshape(1152),
        per_head[1, 0:16],
        per_head[2, 0:16],
        per_head[3, 0:16],
        gate.reshape(1024),
        w_out_grad,
    )


def solution(mesh):
    placed = (
        P(("rep", "grp"), None),
        P(("rep", "grp")),
        P("grp"),
        P("grp", None),
        P(None, "grp"),
        P("grp"),
        P("grp"),
        P("grp"),
        P("grp"),
        P("grp"),
        P("grp", None),
        P(("rep", "grp"), None),
    )
    return jax.shard_map(
        on_device,
        mesh=mesh,
        in_specs=placed,
        out_specs=(
            P(("rep", "grp"), None),
            P(("rep", "grp"), None),
            P("grp"),
            P("grp", None),
            P(None, "grp"),
            P("grp"),
            P("grp"),
            P("grp"),
            P("grp"),
            P("grp"),
            P("grp", None),
        ),
        check_vma=False,
    )
```

time: 1260 us -> 256 us (0.20)
  waiting for transfers between devices: 706 us -> 62.9 us
  blocking collectives: 316 us -> 0 us
  Pallas kernels: 0 us -> 170 us
  matrix products: 96 us -> 0 us
  other arithmetic: 60.1 us -> 3.4 us
  local copies, waits for them, and re-layouts: 40 us -> 4.68 us
    psum x1 -> x0, blocking collectives: 274 us -> none  [on_device(): lax.psum((summed[0], summed[1], summed[2], summed[3], summed[4], summed[5...]
    psum x1, waiting for transfers between devices: 311 us -> 62.9 us  [on_device(): lax.psum(vecs, ('rep', 'grp'))]
    reduce_scatter x2 -> x0, waiting for transfers between devices: 243 us -> none  [the longest x1 207 us: on_device(): lax.psum_scatter(in_grad, 'grp', scatter_dimension=0, tiled=True)]
    pallas_call x0 -> x4, Pallas kernels: none -> 170 us  [the longest x1 75.1 us: reduce_gradients(): pl.pallas_call(reduce_kernel, out_shape=[jax.ShapeDtypeStruct((2, 2, 4, 4...]
    all_gather x4 -> x0, waiting for transfers between devices: 146 us -> none  [the longest x1 88.1 us: on_device(): lax.all_gather(w_in, 'grp', axis=0, tiled=True)]
    dot_general x19 -> x0, matrix products: 96 us -> none  [the longest x3 35.2 us: ssd_block(): output = jnp.einsum('tsh,shd->thd', weights, head_in, precision=HIGHEST)]
    all_gather x6 -> x0, blocking collectives: 28.5 us -> none  [the longest x1 5.03 us: entering(): everything = jax.tree.map(lambda part: lax.all_gather(part, axis), shard)]
    unnamed x228 -> x0, local copies, waits for them, and re-layouts: 25.4 us -> none
  transfers between devices with their start and end apart: 11 -> 1, of which waited for: 7 -> 1; matrix products, arithmetic and copies ran while one was open for 11% -> 0% of each run, Pallas kernels for 0% -> 29%
where the time goes in v2:
time: 256 us; the launch traced here: 255 us
  Pallas kernels  170 us (66%)
  waiting for transfers between devices  62.9 us (25%)
  between operations  14.1 us (6%)
  local copies, waits for them, and re-layouts  4.68 us (2%)
  other arithmetic  3.4 us (1%)
    pallas_call x1, Pallas kernels, reduce_gradients(): pl.pallas_call(reduce_kernel, out_shape=[jax.ShapeDtypeStruct((2, 2, 4, 4...  75.1 us
    psum x1, waiting for transfers between devices, on_device(): lax.psum(vecs, ('rep', 'grp'))  62.9 us
    pallas_call x1, Pallas kernels, layer_grads(): pl.pallas_call(layer_body, out_shape=[shape((OWN, SEQ), bf16), shape((256...  50.2 us
    pallas_call x1, Pallas kernels, gather(): pl.pallas_call(gather_kernel, out_shape=[jax.ShapeDtypeStruct((2560, 1024...  34.3 us
    pallas_call x1, Pallas kernels, finish(): pl.pallas_call(finish_kernel, out_shape=[shape((4384, 512), f32), shape((...  10.6 us
  transfers between devices with their start and end apart: 1, of which 1 were waited for; matrix products, arithmetic and copies ran while one was open for 0% of the time, Pallas kernels for 29%

profile of v2, /device:TPU:1, one launch (start us, length us, event | category | flops | bytes accessed | tf_op | source)
XLA Modules:
  0.0 255.4 jit_solution(812528390454413564)
XLA Ops:
  7.2 0.0 all-reduce.9.cloned.1.call-start
  7.2 0.7 convert_element_type.37
  7.9 0.7 maximum_convert_fusion
  8.6 0.1 pad_select_fusion
  8.7 1.3 add_convert_fusion.small_ref
  10.0 1.3 broadcast_in_dim.2.seg_ref
  11.3 34.3 %gather.1 = (bf16[2560,1024]{1,0:T(8,128)(2,1)}, bf16[2,64,128]{2,1,0:T(8,128)(2,1)}, s32[8,512]{1,0:T(8,128)}, bf16[512,1024]{1,0:T(8,128)(2,1)}) custom-call(bf16[4384,512]{1,0:T(8,128)(2,1)} %bitcast.18, bf16[64,128]{1,0:T(8,128)(2,1)} %add_convert_fusion.small_ref, s32[8,256]{1,0:T(8,128)} %broadcast_in_dim.2.seg_ref, bf16[256,1024]{1,0:T(8,128)(2,1)} %tokens.1), custom_call_target="tpu_custom_call" | custom-call | tf_op jit(solution)/shard_map/gather/pallas_call | solution.py:677
  45.7 50.2 %layer_grads.1 = (bf16[1024,512]{1,0:T(8,128)(2,1)}, bf16[256,1024]{1,0:T(8,128)(2,1)}, bf16[2560,512]{1,0:T(8,128)(2,1)}, bf16[512,1024]{1,0:T(8,128)(2,1)}, bf...) custom-call(bf16[512,1024]{1,0:T(8,128)(2,1)} %get-tuple-element.39., ...), custom_call_target="tpu_custom_call" | custom-call | tf_op jit(solution)/shard_map/layer_grads/pallas_call | solution.py:378
  95.9 0.0 all-reduce.9.cloned.1.call-update
  95.9 75.1 %reduce_gradients.1 = (bf16[2,2,4,4,2,2,80,128]{7,6,5,4,3,2,1,0:T(8,128)(2,1)}, bf16[4,4,2,32,1024]{4,3,2,1,0:T(8,128)(2,1)}, bf16[256,1024]{1,0:T(8,128)(2,1)}) custom-call(bf16[512,1024]{1,0:T(8,128)(2,1)} %get-tuple-element.43.normed_ref, bf16[2560,512]{1,0:T(8,128)(2,1)} %get-tuple-element.44.pg_ref, bf16[1024,512]{1,0:T(8,128)(2,1)} %get-tuple-element.45.branch_ref, ...), custom_call_target="tpu_custom_call" | custom-call | tf_op jit(solution)/shard_map/reduce_gradients/pallas_call | solution.py:975
  171.0 62.9 %all-reduce.9.cloned.1.call-done = f32[2,64,128]{2,1,0:T(8,128)} async-done(((f32[2,64,128]{2,1,0:T(8,128)}), f32[2,64,128]{2,1,0:T(8,128)}) %all-reduce.9.cloned.1.call-update) | async-done | bytes 65552 | tf_op jit(solution)/shard_map/psum | solution.py:1124
  233.9 1.4 dynamic-slice_bitcast_fusion.vecs_ref
  235.2 10.6 %finish.1 = (f32[4384,512]{1,0:T(8,128)}, f32[1024,1024]{1,0:T(8,128)}, f32[256,1024]{1,0:T(8,128)}, bf16[256,1024]{1,0:T(8,128)(2,1)}, f32[4,128]{1,0:T(4,128)}...) custom-call(bf16[2,2,4,4,2,2,80,128]{7,6,5,4,3,2,1,0:T(8,128)(2,1)} %get-tuple-element.53.sum_w, ...), custom_call_target="tpu_custom_call" | custom-call | tf_op jit(solution)/shard_map/finish/pallas_call | solution.py:1069
  245.9 1.3 slice_bitcast_fusion
  247.2 1.3 reduce
Async XLA Ops:
  7.2 226.7 %all-reduce.9.cloned.1.call-start = ((), (), s32[]{:S(2)}) async-start(), calls=%async_computation | async-start | bytes 131072 | tf_op jit(solution)/shard_map/psum | solution.py:1124
Sparse Core Ops, SparseCore 0:
  96.0 137.8 all-reduce.8
